TPU v7x, 32 devices: a whole 2x2x4 slice. The times are simulated.
32 devices in a mesh: grp: 4 (over y, x), dev: 8 (over z, core).
Axes of the slice: x: 2, y: 2, z: 4, core: 2. Of those that a mesh axis runs over, the one named last changes fastest.
Arguments:
- queries: bfloat16 [32, 3072], P(('grp', 'dev')), may hold values from -480 to 480
- cached_key_rows: bfloat16 [32, 512, 512], P(('grp', 'dev')), may hold values from -6 to 6
- cached_value_rows: bfloat16 [32, 512, 512], P(('grp', 'dev')), may hold values from -6 to 6
- incoming_keys: bfloat16 [32, 512], P(('grp', 'dev')), may hold values from -6 to 6
- incoming_values: bfloat16 [32, 512], P(('grp', 'dev')), may hold values from -6 to 6
- lengths: int32 [16], P('grp'), may hold values from 64 to 512, as said below
- residual: bfloat16 [16, 6144], P('grp'), may hold values from -6 to 6
- norm_gain: float32 [6144], replicated, may hold values from 0.25 to 1.75
- expert_ids: int32 [16, 2], P('grp'), may hold values from 0 to 7, all different within a row; in each aligned block of 4 rows (0 to 3, 4 to 7, ...) at most 4 rows name the same one
- route_logits: float32 [16, 2], P('grp'), may hold values from -6 to 6
- w_gate: bfloat16 [6144, 65536], P(None, ('dev', 'grp')), may hold values from -0.078125 to 0.078125
- w_up: bfloat16 [6144, 65536], P(None, ('dev', 'grp')), may hold values from -0.078125 to 0.078125
- w_down: bfloat16 [65536, 6144], P(('dev', 'grp')), may hold values from -0.0625 to 0.0625
Outputs:
- moe_out: bfloat16 [16, 6144], P('grp', 'dev')
Inputs may be any that keep to these rules, and one draw needn't show every extreme that they name: `lengths`: A sequence has at least 64 live positions; some sequence has exactly 512. `expert_ids`: each token names 2 different experts; among the tokens of one group (4 aligned rows) no expert is named more than 4 times, a bound that some block reaches.
All inputs are finite; a program needn't handle non-finite values.
Results may differ from a plain program's by a relative error of at most 0.007.
Values may be sent and summed in bfloat16 or wider, within the bound.
No kernel may reach another device: no remote copies, remote signals or barrier semaphores. Data moves between devices by JAX's collectives and lax.ppermute only.
A program may use at most 192 MiB of HBM per device.

v0:
```python
import jax
import jax.numpy as jnp
from jax import lax
from jax.sharding import PartitionSpec as P

QUERY_HEADS = 48
KEY_VALUE_HEADS = 8
HEAD_SIZE = 128
E = 8
SHARING_DEVICES = 2


def slot_matrix(id_rows, prob_rows, expert, slot_cap):
    matched = (id_rows == expert).astype(jnp.int32).reshape(-1)
    position = jnp.cumsum(matched) - matched
    slot_hit = (position[None, :] == jnp.arange(slot_cap, dtype=jnp.int32)[:, None]) & (
        matched[None, :] > 0
    )
    slot_hit = slot_hit.astype(jnp.float32).reshape(slot_cap, id_rows.shape[0], id_rows.shape[1])
    return (jnp.sum(slot_hit, axis=2), jnp.sum(slot_hit * prob_rows[None], axis=(1, 2)))


def body(
    queries,
    cached_key_rows,
    cached_value_rows,
    incoming_keys,
    incoming_values,
    lengths,
    residual,
    norm_gain,
    expert_ids,
    route_logits,
    w_gate,
    w_up,
    w_down,
):
    dev_count = lax.axis_size("dev")
    head_local = cached_key_rows.shape[2] // HEAD_SIZE
    query_group_width = QUERY_HEADS // KEY_VALUE_HEADS
    cache_len = cached_key_rows.shape[1]
    score_scale = HEAD_SIZE ** (-0.5)
    seq_here = lax.axis_index("dev") // SHARING_DEVICES
    length_row = lax.dynamic_slice_in_dim(lengths, seq_here, 1)[0]
    query_mat = queries[0].reshape(head_local, query_group_width, HEAD_SIZE)
    key_mat = cached_key_rows[0].reshape(cache_len, head_local, HEAD_SIZE)
    value_mat = cached_value_rows[0].reshape(cache_len, head_local, HEAD_SIZE)
    score_all = (
        jnp.einsum("hgd,thd->hgt", query_mat, key_mat, preferred_element_type=jnp.float32)
        * score_scale
    )
    mask_live = jnp.arange(cache_len, dtype=jnp.int32) < length_row
    score_all = jnp.where(mask_live[None, None, :], score_all, -1e30)
    new_score = (
        jnp.einsum(
            "hgd,hd->hg",
            query_mat,
            incoming_keys[0].reshape(head_local, HEAD_SIZE),
            preferred_element_type=jnp.float32,
        )
        * score_scale
    )
    row_max = jnp.maximum(jnp.max(score_all, axis=-1), new_score)
    exp_all = jnp.exp(score_all - row_max[..., None])
    exp_new = jnp.exp(new_score - row_max)
    denom_all = jnp.sum(exp_all, axis=-1) + exp_new
    attn_weights = (exp_all / denom_all[..., None]).astype(jnp.bfloat16)
    weight_new = (exp_new / denom_all).astype(jnp.bfloat16)
    mixed_out = jnp.einsum(
        "hgt,thd->hgd", attn_weights, value_mat, preferred_element_type=jnp.float32
    )
    mixed_out = mixed_out + weight_new.astype(jnp.float32)[..., None] * incoming_values[0].reshape(
        head_local, 1, HEAD_SIZE
    ).astype(jnp.float32)
    attended = mixed_out.reshape(1, -1).astype(jnp.bfloat16)
    gathered = lax.all_gather(attended, "dev", axis=0, tiled=True)
    heads_all = gathered.reshape(residual.shape)
    summed = residual.astype(jnp.float32) + heads_all.astype(jnp.float32)
    normed = (
        summed * lax.rsqrt(jnp.mean(summed * summed, axis=-1, keepdims=True) + 1e-05) * norm_gain
    ).astype(jnp.bfloat16)
    route_probs = jax.nn.softmax(route_logits, axis=-1)
    expert = lax.axis_index("dev") // (dev_count // E)
    row_cap = min(10, dev_count // SHARING_DEVICES)
    select_all, slot_weight = slot_matrix(expert_ids, route_probs, expert, row_cap)
    picked = jnp.dot(
        select_all.astype(jnp.bfloat16), normed, preferred_element_type=jnp.float32
    ).astype(jnp.bfloat16)
    rows_all = lax.all_gather(picked, "grp", axis=0, tiled=True)
    gate_out = jnp.dot(rows_all, w_gate, preferred_element_type=jnp.float32)
    up_out = jnp.dot(rows_all, w_up, preferred_element_type=jnp.float32)
    hidden = (jax.nn.silu(gate_out) * up_out).astype(jnp.bfloat16)
    columns = lax.all_to_all(w_down, "grp", split_axis=1, concat_axis=0, tiled=True)
    partial_out = jnp.dot(
        lax.all_gather(hidden, "grp", axis=1, tiled=True),
        columns,
        preferred_element_type=jnp.float32,
    )
    expert_out = lax.all_to_all(partial_out, "grp", split_axis=0, concat_axis=1, tiled=True)
    contrib = jnp.dot(
        select_all.T, slot_weight[:, None] * expert_out, precision=lax.Precision.HIGHEST
    )
    return lax.psum_scatter(contrib, "dev", scatter_dimension=1, tiled=True).astype(jnp.bfloat16)


def solution(mesh):
    return jax.shard_map(
        body,
        mesh=mesh,
        in_specs=(
            P(("grp", "dev"), None),
            P(("grp", "dev"), None, None),
            P(("grp", "dev"), None, None),
            P(("grp", "dev"), None),
            P(("grp", "dev"), None),
            P("grp"),
            P("grp", None),
            P(),
            P("grp", None),
            P("grp", None),
            P(None, ("dev", "grp")),
            P(None, ("dev", "grp")),
            P(("dev", "grp"), None),
        ),
        out_specs=P("grp", "dev"),
        check_vma=False,
    )
```

profile of v0, /device:TPU:1, one launch (start us, length us, event | category | flops | bytes accessed | tf_op | source)
XLA Modules:
  0.0 411.9 jit_solution(8303354270660223148)
XLA Ops:
  6.5 0.0 copy-start
  6.5 20.5 %copy.47 = bf16[256,4,8,1536]{3,2,0,1:T(8,128)(2,1)} copy(bf16[256,4,8,1536]{3,2,1,0:T(8,128)(2,1)} %bitcast.34) | data formatting | bytes 50331648 | tf_op jit(solution)/shard_map/all_to_all | solution.py:93
  27.1 0.0 copy-start.6
  27.1 0.0 copy-start.7
  27.1 0.0 copy-start.4
  27.1 0.0 copy-start.1
  27.1 0.0 copy-start.2
  27.1 0.0 copy-start.9
  27.1 0.0 copy-start.5
  27.1 0.0 copy-start.3
  27.1 0.0 copy-start.8
  27.1 8.6 %all-to-all-start = ((bf16[2048,4,1536]{2,0,1:T(8,128)(2,1)}), bf16[2048,4,1536]{2,0,1:T(8,128)(2,1)}, u32[]{:S(2)}, u32[]{:S(2)}) async-start(bf16[2048,4,1536]{2,0,1:T(8,128)(2,1)} %bitcast.33), calls=%async_computation | async-start | bytes 50331648 | tf_op jit(solution)/shard_map/all_to_all | solution.py:93
  35.7 0.0 reduce-scatter.4.cloned.1.call-start
  35.8 0.0 copy-done.6
  35.8 0.0 copy-done.7
  35.8 0.1 copy.29
  35.9 0.1 copy.31
  36.0 0.1 reshape.90
  36.1 0.2 reduce-window_clone.1
  36.3 0.5 broadcast.81
  36.8 0.7 reduce.6
  37.5 0.1 reshape.91
  37.5 0.1 copy.30
  37.6 0.0 copy-done.4
  37.7 0.0 copy-done.1
  37.7 0.1 reshape_squeeze.14
  37.8 0.0 copy-done.2
  37.9 0.1 reshape_squeeze.16
  38.0 0.0 copy-done.9
  38.0 0.6 dynamic_slice.3
  38.6 0.6 iota_compare_fusion.1
  39.2 0.0 copy-done
  39.3 0.1 fusion.14
  39.4 0.3 fusion.21
  39.7 0.2 fusion.7
  39.9 0.2 fusion.3
  40.2 15.5 %all-gather = bf16[8,1,3072]{2,1,0:T(2,128)(2,1)S(1)} all-gather(bf16[1,1,3072]{2,1,0:T(2,128)(2,1)S(1)} %reshape.94), channel_id=1, replica_groups=mesh['grp'=4,'dev'=8] {'dev'}, dimensions={0}, use_global_device_ids=true | all-gather | bytes 55296 | tf_op jit(solution)/shard_map/all_gather | solution.py:76
  55.6 0.3 convert_reduce_fusion
  56.0 0.0 copy-done.5
  56.0 0.1 select_reduce_fusion
  56.2 0.0 copy-done.3
  56.2 0.2 multiply_reduce_fusion
  56.3 0.0 copy-done.8
  56.4 0.2 fusion
  56.6 254.7 %all-gather.1 = bf16[4,4,6144]{2,1,0:T(4,128)(2,1)S(1)} all-gather(bf16[1,4,6144]{2,1,0:T(4,128)(2,1)S(1)} %fusion), channel_id=1, replica_groups=mesh['grp'=4,'dev'=8] {'grp'}, dimensions={0}, use_global_device_ids=true | all-gather | bytes 245760 | tf_op jit(solution)/shard_map/all_gather | solution.py:89
  311.4 9.9 %fusion.22 = f32[16,2048]{1,0:T(8,128)S(1)} fusion(bf16[16,6144]{1,0:T(8,128)(2,1)S(1)} %reshape.97, bf16[6144,2048]{1,0:T(8,128)(2,1)} %param.23), kind=kOutput, calls=%fused_computation.45 | convolution fusion | flops 402653184 | bytes 25493504 | tf_op jit(solution)/shard_map/dot_general | solution.py:90
  321.3 10.0 %fusion.1 = bf16[16,2048]{1,0:T(8,128)(2,1)S(1)} fusion(bf16[16,6144]{1,0:T(8,128)(2,1)S(1)} %reshape.97, bf16[6144,2048]{1,0:T(8,128)(2,1)} %param.24, f32[16,2048]{1,0:T(8,128)S(1)} %fusion.22), kind=kOutput, calls=%fused_computation.5 | convolution fusion | flops 402849792 | bytes 25559040 | tf_op jit(solution)/shard_map/dot_general | solution.py:91
  331.2 6.0 %all_gather.11 = bf16[16,8192]{1,0:T(8,128)(2,1)S(1)} all-gather(bf16[16,2048]{1,0:T(8,128)(2,1)S(1)} %fusion.1), channel_id=1, replica_groups=mesh['grp'=4,'dev'=8] {'grp'}, dimensions={1}, use_global_device_ids=true | all-gather | bytes 327680 | tf_op jit(solution)/shard_map/all_gather | solution.py:95
  337.3 0.1 dot_general.32
  337.4 0.0 all-to-all-done
  337.4 10.1 %fusion.23 = f32[4,4,1536]{2,1,0:T(4,128)S(1)} fusion(bf16[4,4,8192]{2,1,0:T(4,128)(2,1)S(1)} %dot_general.32, bf16[8192,1536,1]{1,0,2:T(8,128)(2,1)} %bitcast.8), kind=kOutput, calls=%fused_computation.46 | convolution fusion | flops 402653184 | bytes 25526272 | tf_op jit(solution)/shard_map/dot_general | solution.py:94
  347.5 6.4 %all_to_all.35 = f32[4,4,1536]{2,1,0:T(4,128)S(1)} all-to-all(f32[4,4,1536]{2,1,0:T(4,128)S(1)} %fusion.23), channel_id=1, replica_groups=mesh['grp'=4,'dev'=8] {'grp'}, dimensions={0} | all-to-all | bytes 196608 | tf_op jit(solution)/shard_map/all_to_all | solution.py:99
  353.8 6.8 %convolution_bitcast_fusion = f32[6144,4]{1,0:T(8,128)} fusion(f32[4,4]{1,0:T(4,128)S(1)} %get-tuple-element.6, f32[4,6144]{1,0:T(4,128)S(1)} %bitcast.35, f32[4]{0:T(128)S(1)} %get-tuple-element.5), kind=kOutput, calls=%fused_computation.1 | convolution fusion | flops 1204224 | bytes 196688
  360.6 0.0 reduce-scatter.4.cloned.1.call-update
  360.7 42.7 %reduce-scatter.4.cloned.1.call-done = f32[768,4]{1,0:T(8,128)} async-done(((f32[6144,4]{1,0:T(8,128)}), f32[768,4]{1,0:T(8,128)}) %reduce-scatter.4.cloned.1.call-update) | async-done | bytes 12304
  403.3 1.7 copy.38
  (14 shorter events, 0.3 us)
Async XLA Ops:
  6.5 32.7 %copy-start = (bf16[1,512]{1,0:T(2,128)(2,1)S(1)}, bf16[1,512]{1,0:T(2,128)(2,1)}, u32[]{:S(2)}) copy-start(bf16[1,512]{1,0:T(2,128)(2,1)} %param.16) | copy-start | bytes 3076
  27.1 8.7 %copy-start.6 = (bf16[1,512]{1,0:T(2,128)(2,1)S(1)}, bf16[1,512]{1,0:T(2,128)(2,1)}, u32[]{:S(2)}) copy-start(bf16[1,512]{1,0:T(2,128)(2,1)} %param.17) | copy-start | bytes 3076
  27.1 8.7 %copy-start.7 = (s32[4,2]{0,1:T(2,128)S(1)}, s32[4,2]{0,1:T(2,128)}, u32[]{:S(2)}) copy-start(s32[4,2]{0,1:T(2,128)} %param.21) | copy-start | bytes 100
  27.1 10.6 %copy-start.4 = (bf16[1,3072]{1,0:T(2,128)(2,1)S(1)}, bf16[1,3072]{1,0:T(2,128)(2,1)}, u32[]{:S(2)}) copy-start(bf16[1,3072]{1,0:T(2,128)(2,1)} %param.13) | copy-start | bytes 18436
  27.1 10.6 %copy-start.1 = (bf16[1,512,512]{2,1,0:T(8,128)(2,1)S(1)}, bf16[1,512,512]{2,1,0:T(8,128)(2,1)}, u32[]{:S(2)}) copy-start(bf16[1,512,512]{2,1,0:T(8,128)(2,1)} %param.14) | copy-start | bytes 1572868
  27.1 10.8 %copy-start.2 = (bf16[1,512,512]{2,1,0:T(8,128)(2,1)S(1)}, bf16[1,512,512]{2,1,0:T(8,128)(2,1)}, u32[]{:S(2)}) copy-start(bf16[1,512,512]{2,1,0:T(8,128)(2,1)} %param.15) | copy-start | bytes 1572868
  27.1 10.9 %copy-start.9 = (s32[4]{0:T(128)S(1)}, s32[4]{0:T(128)}, u32[]{:S(2)}) copy-start(s32[4]{0:T(128)} %param.18) | copy-start | bytes 52
  27.1 28.9 %copy-start.5 = (f32[4,2]{0,1:T(2,128)S(1)}, f32[4,2]{0,1:T(2,128)}, u32[]{:S(2)}) copy-start(f32[4,2]{0,1:T(2,128)} %param.22) | copy-start | bytes 100
  27.1 29.1 %copy-start.3 = (bf16[4,6144]{1,0:T(4,128)(2,1)S(1)}, bf16[4,6144]{1,0:T(4,128)(2,1)}, u32[]{:S(2)}) copy-start(bf16[4,6144]{1,0:T(4,128)(2,1)} %param.19) | copy-start | bytes 147460
  27.1 29.2 %copy-start.8 = (f32[6144]{0:T(1024)S(1)}, f32[6144]{0:T(1024)}, u32[]{:S(2)}) copy-start(f32[6144]{0:T(1024)} %param.20) | copy-start | bytes 73732
  27.1 310.3 %all-to-all-start = ((bf16[2048,4,1536]{2,0,1:T(8,128)(2,1)}), bf16[2048,4,1536]{2,0,1:T(8,128)(2,1)}, u32[]{:S(2)}, u32[]{:S(2)}) async-start(bf16[2048,4,1536]{2,0,1:T(8,128)(2,1)} %bitcast.33), calls=%async_computation | async-start | bytes 50331648 | tf_op jit(solution)/shard_map/all_to_all | solution.py:93
  35.7 367.6 %reduce-scatter.4.cloned.1.call-start = ((), (), s32[]{:S(2)}) async-start(), calls=%async_computation.3 | async-start | bytes 3538944
Sparse Core Ops, SparseCore 0:
  360.8 42.5 reduce-scatter.3
where the time goes:
time: 416 us; the launch traced here: 412 us
  blocking collectives  283 us (68%)
  waiting for transfers between devices  42.7 us (10%)
  matrix products  37.7 us (9%)
  local copies, waits for them, and re-layouts  24.4 us (6%)
  between operations  13.6 us (3%)
  starting transfers between devices  8.61 us (2%)
    all_gather x1, blocking collectives, body(): rows_all = lax.all_gather(picked, 'grp', axis=0, tiled=True)  255 us
    unnamed x2, waiting for transfers between devices  42.7 us
    all_to_all x1, local copies, waits for them, and re-layouts, body(): lax.all_to_all(w_down, 'grp', split_axis=1, concat_axis=0, tiled=True)  20.5 us
    all_gather x1, blocking collectives, body(): gathered = lax.all_gather(attended, 'dev', axis=0, tiled=True)  15.5 us
    dot_general x1, matrix products, body(): jnp.dot(lax.all_gather(hidden, 'grp', axis=1, tiled=True), columns, prefe...  10.1 us
    dot_general x1, matrix products, body(): up_out = jnp.dot(rows_all, w_up, preferred_element_type=jnp.float32)  9.96 us
    dot_general x1, matrix products, body(): gate_out = jnp.dot(rows_all, w_gate, preferred_element_type=jnp.float32)  9.91 us
    all_to_all x1, starting transfers between devices, body(): lax.all_to_all(w_down, 'grp', split_axis=1, concat_axis=0, tiled=True)  8.57 us
  transfers between devices with their start and end apart: 2, of which 1 were waited for; matrix products, arithmetic and copies ran while one was open for 6% of the time, Pallas kernels for 0%

commit v1 on v0

v1 whole, which is shorter than its diff:
```python
import functools

import jax
import jax.numpy as jnp
from jax import lax
from jax.experimental import pallas as pl
from jax.experimental.pallas import tpu as pltpu
from jax.sharding import PartitionSpec as P

QUERY_HEADS = 48
KEY_VALUE_HEADS = 8
HEAD_SIZE = 128
E = 8
SHARING_DEVICES = 2
GROUP_WIDTH = QUERY_HEADS // KEY_VALUE_HEADS
LOCAL_HEADS = QUERY_HEADS // SHARING_DEVICES
MIB = 2**20
VMEM = pl.BlockSpec(memory_space=pltpu.VMEM)
SMEM = pl.BlockSpec(memory_space=pltpu.SMEM)
ANY = pl.BlockSpec(memory_space=pl.ANY)


def head_rows(row):
    heads = row.shape[1] // HEAD_SIZE
    return jnp.concatenate(
        [row[:, j * HEAD_SIZE : (j + 1) * HEAD_SIZE] for j in range(heads)], axis=0
    )


def attend_kernel(
    lengths, queries, key_rows, value_rows, new_keys, new_values, residual, out
):
    position = lax.axis_index("dev")
    sequence = lax.div(position, SHARING_DEVICES)
    half = lax.rem(position, SHARING_DEVICES)
    heads, cache_len = LOCAL_HEADS, key_rows.shape[1]
    width = key_rows.shape[2]
    kv_heads = width // HEAD_SIZE
    scale = HEAD_SIZE ** (-0.5)
    query = head_rows(queries[...].astype(jnp.float32))
    owner = lax.broadcasted_iota(jnp.int32, (heads, HEAD_SIZE), 0) // GROUP_WIDTH
    blocks = [jnp.where(owner == b, query, 0.0) for b in range(kv_heads)]
    spread = jnp.concatenate(blocks, axis=1)
    scores = (
        lax.dot_general(
            spread.astype(jnp.bfloat16),
            key_rows[0],
            (((1,), (1,)), ((), ())),
            preferred_element_type=jnp.float32,
        )
        * scale
    )
    places = lax.broadcasted_iota(jnp.int32, (heads, cache_len), 1)
    scores = jnp.where(places < lengths[sequence], scores, -1e30)
    new_score = (
        jnp.sum(spread * new_keys[...].astype(jnp.float32), axis=1, keepdims=True) * scale
    )
    row_max = jnp.maximum(jnp.max(scores, axis=1, keepdims=True), new_score)
    exp_all = jnp.exp(scores - row_max)
    exp_new = jnp.exp(new_score - row_max)
    denom = jnp.sum(exp_all, axis=1, keepdims=True) + exp_new
    weights = (exp_all / denom).astype(jnp.bfloat16)
    weight_new = (exp_new / denom).astype(jnp.bfloat16).astype(jnp.float32)
    mixed = jnp.dot(weights, value_rows[0], preferred_element_type=jnp.float32)
    mixed = mixed + weight_new * new_values[...].astype(jnp.float32)
    attended = jnp.zeros((heads, HEAD_SIZE), jnp.float32)
    for b in range(kv_heads):
        attended = jnp.where(
            owner == b, mixed[:, b * HEAD_SIZE : (b + 1) * HEAD_SIZE], attended
        )
    attended = attended.astype(jnp.bfloat16).astype(jnp.float32)
    columns = heads * HEAD_SIZE
    mine = residual[:, pl.ds(pl.multiple_of(half * columns, HEAD_SIZE), columns)].astype(jnp.float32)
    rows = lax.broadcasted_iota(jnp.int32, mine.shape, 0)
    mine = jnp.sum(jnp.where(rows == sequence, mine, 0.0), axis=0, keepdims=True)
    summed = (attended + head_rows(mine)).astype(jnp.bfloat16)
    out[...] = jnp.broadcast_to(summed[None], out.shape)


def attend(lengths, queries, key_rows, value_rows, new_keys, new_values, residual, devices):
    return pl.pallas_call(
        attend_kernel,
        out_shape=jax.ShapeDtypeStruct((devices, LOCAL_HEADS, HEAD_SIZE), jnp.bfloat16),
        in_specs=[SMEM] + [VMEM] * 6,
        out_specs=VMEM,
        compiler_params=pltpu.CompilerParams(vmem_limit_bytes=24 * MIB),
        name="attend",
    )(lengths, queries, key_rows, value_rows, new_keys, new_values, residual)


def experts_kernel(
    parts, gain, w_gate, w_up, w_down, out,
    flat, normed, hidden, gate_buf, up_buf, down_buf, gate_sem, up_sem, down_sem,
):
    devices = parts.shape[0]
    tokens, width = normed.shape
    ring, _, tile = gate_buf.shape
    tiles = w_gate.shape[1] // tile
    columns = out.shape[2]
    slices = w_down.shape[1] // columns
    down_ring = down_buf.shape[0]

    def copies(n):
        at = pl.ds(pl.multiple_of(n * tile, tile), tile)
        slot = lax.rem(n, ring)
        return (
            pltpu.make_async_copy(w_gate.at[:, at], gate_buf.at[slot], gate_sem.at[slot]),
            pltpu.make_async_copy(w_up.at[:, at], up_buf.at[slot], up_sem.at[slot]),
        )

    def down_copy(n):
        at = pl.ds(pl.multiple_of(n * columns, HEAD_SIZE), columns)
        slot = lax.rem(n, down_ring)
        return pltpu.make_async_copy(w_down.at[:, at], down_buf.at[slot], down_sem.at[slot])

    for n in range(min(ring, tiles)):
        for copy in copies(n):
            copy.start()
    for n in range(min(down_ring, slices)):
        down_copy(n).start()

    flat[...] = parts[...].astype(jnp.float32).reshape(flat.shape)
    heads = width // HEAD_SIZE
    square = jnp.zeros((tokens, HEAD_SIZE), jnp.float32)
    for j in range(heads):
        piece = flat[pl.ds(j, tokens, stride=heads), :]
        square = square + piece * piece
    mean = jnp.sum(square, axis=1, keepdims=True) * (1.0 / width)
    inverse = lax.rsqrt(mean + 1e-05)
    for j in range(heads):
        piece = flat[pl.ds(j, tokens, stride=heads), :]
        normed[:, j * HEAD_SIZE : (j + 1) * HEAD_SIZE] = (
            piece * inverse * gain[j : j + 1, :]
        ).astype(jnp.bfloat16)

    def gate_step(n, carry):
        slot = lax.rem(n, ring)
        for copy in copies(n):
            copy.wait()
        gate = jnp.dot(normed[...], gate_buf[slot], preferred_element_type=jnp.float32)
        up = jnp.dot(normed[...], up_buf[slot], preferred_element_type=jnp.float32)
        at = pl.ds(pl.multiple_of(n * tile, tile), tile)
        hidden[:, at] = (gate / (1.0 + jnp.exp(-gate)) * up).astype(jnp.bfloat16)

        @pl.when(n + ring < tiles)
        def _():
            for copy in copies(n + ring):
                copy.start()

        return carry

    lax.fori_loop(0, tiles, gate_step, 0)

    group_rows = out.shape[1]

    def down_step(n, carry):
        slot = lax.rem(n, down_ring)
        down_copy(n).wait()
        part = jnp.dot(hidden[...], down_buf[slot], preferred_element_type=jnp.float32)
        for g in range(tokens // group_rows):
            out[g * slices + n] = part[g * group_rows : (g + 1) * group_rows].astype(out.dtype)

        @pl.when(n + down_ring < slices)
        def _():
            down_copy(n + down_ring).start()

        return carry

    lax.fori_loop(0, slices, down_step, 0)


def experts(parts, gain, w_gate, w_up, w_down, group_rows, dev_count):
    devices = parts.shape[0]
    width, local_hidden = w_gate.shape
    tokens = devices * LOCAL_HEADS * HEAD_SIZE // width
    tile, ring, down_ring = 512, 2, 6
    columns = width // dev_count
    return pl.pallas_call(
        experts_kernel,
        out_shape=jax.ShapeDtypeStruct((devices, group_rows, columns), jnp.bfloat16),
        in_specs=[VMEM, VMEM, ANY, ANY, ANY],
        out_specs=VMEM,
        scratch_shapes=[
            pltpu.VMEM((devices * LOCAL_HEADS, HEAD_SIZE), jnp.float32),
            pltpu.VMEM((tokens, width), jnp.bfloat16),
            pltpu.VMEM((tokens, local_hidden), jnp.bfloat16),
            pltpu.VMEM((ring, width, tile), jnp.bfloat16),
            pltpu.VMEM((ring, width, tile), jnp.bfloat16),
            pltpu.VMEM((down_ring, local_hidden, columns), jnp.bfloat16),
            pltpu.SemaphoreType.DMA((ring,)),
            pltpu.SemaphoreType.DMA((ring,)),
            pltpu.SemaphoreType.DMA((down_ring,)),
        ],
        compiler_params=pltpu.CompilerParams(vmem_limit_bytes=56 * MIB),
        name="experts",
    )(parts, gain.reshape(width // HEAD_SIZE, HEAD_SIZE), w_gate, w_up, w_down)


def experts_plain(parts, gain, w_gate, w_up, w_down, group_rows, dev_count):
    devices = parts.shape[0]
    width = w_gate.shape[0]
    summed = parts.reshape(-1, width).astype(jnp.float32)
    normed = (
        summed * lax.rsqrt(jnp.mean(summed * summed, axis=-1, keepdims=True) + 1e-05) * gain
    ).astype(jnp.bfloat16)
    gate = jnp.dot(normed, w_gate, preferred_element_type=jnp.float32)
    up = jnp.dot(normed, w_up, preferred_element_type=jnp.float32)
    hidden = (jax.nn.silu(gate) * up).astype(jnp.bfloat16)
    part = jnp.dot(hidden, w_down, preferred_element_type=jnp.float32).astype(jnp.bfloat16)
    part = part.reshape(-1, group_rows, dev_count, width // dev_count)
    return part.transpose(0, 2, 1, 3).reshape(devices, group_rows, -1)


def combine_kernel(per_expert, dev_count, parts, ids, logits, out):
    shards = parts.shape[0] // dev_count
    logit = logits[...]
    top = jnp.max(logit, axis=1, keepdims=True)
    raised = jnp.exp(logit - top)
    probs = raised / jnp.sum(raised, axis=1, keepdims=True)
    chosen = ids[...]
    total = jnp.zeros(out.shape, jnp.float32)
    for e in range(E):
        weight = jnp.sum(jnp.where(chosen == e, probs, 0.0), axis=1, keepdims=True)
        here = jnp.zeros(out.shape, jnp.float32)
        for g in range(shards):
            for c in range(per_expert):
                here = here + parts[g * dev_count + e * per_expert + c].astype(jnp.float32)
        total = total + weight * here
    out[...] = total.astype(out.dtype)


def combine(parts, ids, logits, dev_count):
    return pl.pallas_call(
        functools.partial(combine_kernel, dev_count // E, dev_count),
        out_shape=jax.ShapeDtypeStruct(parts.shape[1:], jnp.bfloat16),
        in_specs=[VMEM] * 3,
        out_specs=VMEM,
        compiler_params=pltpu.CompilerParams(vmem_limit_bytes=24 * MIB),
        name="combine",
    )(parts, ids, logits)


def body(
    queries,
    cached_key_rows,
    cached_value_rows,
    incoming_keys,
    incoming_values,
    lengths,
    residual,
    norm_gain,
    expert_ids,
    route_logits,
    w_gate,
    w_up,
    w_down,
):
    dev_count = lax.axis_size("dev")
    devices = lax.axis_size("grp") * dev_count
    group_rows = residual.shape[0]
    sent = attend(
        lengths, queries, cached_key_rows, cached_value_rows, incoming_keys, incoming_values,
        residual, devices,
    )
    rows = lax.all_to_all(sent, ("grp", "dev"), 0, 0, tiled=True)
    run_experts = experts if w_gate.shape[1] % 512 == 0 else experts_plain
    part = run_experts(rows, norm_gain, w_gate, w_up, w_down, group_rows, dev_count)
    got = lax.all_to_all(part, ("grp", "dev"), 0, 0, tiled=True)
    return combine(got, expert_ids, route_logits, dev_count)


def solution(mesh):
    return jax.shard_map(
        body,
        mesh=mesh,
        in_specs=(
            P(("grp", "dev"), None),
            P(("grp", "dev"), None, None),
            P(("grp", "dev"), None, None),
            P(("grp", "dev"), None),
            P(("grp", "dev"), None),
            P("grp"),
            P("grp", None),
            P(),
            P("grp", None),
            P("grp", None),
            P(None, ("dev", "grp")),
            P(None, ("dev", "grp")),
            P(("dev", "grp"), None),
        ),
        out_specs=P("grp", "dev"),
        check_vma=False,
    )
```

time: 416 us -> 64.7 us (0.16)
  blocking collectives: 283 us -> 16.3 us
  matrix products: 37.7 us -> 0 us
  waiting for transfers between devices: 42.7 us -> 8.94 us
  Pallas kernels: 0 us -> 30.9 us
  local copies, waits for them, and re-layouts: 24.4 us -> 5.8 us
  between operations: 13.6 us -> 0.04 us
  starting transfers between devices: 8.61 us -> 2.34 us
    all_gather x3 -> x0, blocking collectives: 276 us -> none  [the longest x1 255 us: body(): rows_all = lax.all_gather(picked, 'grp', axis=0, tiled=True)]
    unnamed x2 -> x0, waiting for transfers between devices: 42.7 us -> none
    pallas_call x0 -> x3, Pallas kernels: none -> 30.9 us  [the longest x1 28.9 us: experts(): pl.pallas_call(experts_kernel, out_shape=jax.ShapeDtypeStruct((devices, g...]
    dot_general x7 -> x0, matrix products: 30.9 us -> none  [the longest x1 10.1 us: body(): jnp.dot(lax.all_gather(hidden, 'grp', axis=1, tiled=True), columns, prefe...]
    all_to_all x1 -> x0, local copies, waits for them, and re-layouts: 20.5 us -> none  [body(): lax.all_to_all(w_down, 'grp', split_axis=1, concat_axis=0, tiled=True)]
    all_to_all x1, blocking collectives: 6.36 us -> 16.3 us  [body(): rows = lax.all_to_all(sent, ('grp', 'dev'), 0, 0, tiled=True)]
    all_to_all x1, waiting for transfers between devices: 0.01 us -> 8.94 us  [body(): got = lax.all_to_all(part, ('grp', 'dev'), 0, 0, tiled=True)]
    unnamed x1 -> x0, matrix products: 6.8 us -> none
  transfers between devices with their start and end apart: 2 -> 1, of which waited for: 1 -> 1; matrix products, arithmetic and copies ran while one was open for 6% -> 0% of each run, Pallas kernels for 0% -> 0%
where the time goes in v1:
time: 64.7 us; the launch traced here: 64.3 us
  Pallas kernels  30.9 us (48%)
  blocking collectives  16.3 us (25%)
  waiting for transfers between devices  8.94 us (14%)
  local copies, waits for them, and re-layouts  5.8 us (9%)
  starting transfers between devices  2.34 us (4%)
    pallas_call x1, Pallas kernels, experts(): pl.pallas_call(experts_kernel, out_shape=jax.ShapeDtypeStruct((devices, g...  28.9 us
    all_to_all x1, blocking collectives, body(): rows = lax.all_to_all(sent, ('grp', 'dev'), 0, 0, tiled=True)  16.3 us
    all_to_all x1, waiting for transfers between devices, body(): got = lax.all_to_all(part, ('grp', 'dev'), 0, 0, tiled=True)  8.94 us
    unnamed x20, local copies, waits for them, and re-layouts  5.8 us
    all_to_all x1, starting transfers between devices, body(): got = lax.all_to_all(part, ('grp', 'dev'), 0, 0, tiled=True)  2.34 us
  transfers between devices with their start and end apart: 1, of which 1 were waited for; matrix products, arithmetic and copies ran while one was open for 0% of the time, Pallas kernels for 0%

profile of v1, /device:TPU:1, one launch (start us, length us, event | category | flops | bytes accessed | tf_op | source)
XLA Modules:
  0.0 64.3 jit_solution(6332219042782582435)
XLA Ops:
  0.0 0.0 copy-start
  0.0 1.0 %copy-done = bf16[1,512,512]{2,1,0:T(8,128)(2,1)S(1)} copy-done((bf16[1,512,512]{2,1,0:T(8,128)(2,1)S(1)}, bf16[1,512,512]{2,1,0:T(8,128)(2,1)}, u32[]{:S(2)}) %copy-start) | copy-done | bytes 524312
  1.0 0.0 copy-start.1
  1.0 1.0 %copy-done.1 = bf16[1,512,512]{2,1,0:T(8,128)(2,1)S(1)} copy-done((bf16[1,512,512]{2,1,0:T(8,128)(2,1)S(1)}, bf16[1,512,512]{2,1,0:T(8,128)(2,1)}, u32[]{:S(2)}) %copy-start.1) | copy-done | bytes 524312
  2.1 0.0 copy-start.2
  2.1 0.8 %copy-done.2 = bf16[4,6144]{1,0:T(4,128)(2,1)S(1)} copy-done((bf16[4,6144]{1,0:T(4,128)(2,1)S(1)}, bf16[4,6144]{1,0:T(4,128)(2,1)}, u32[]{:S(2)}) %copy-start.2) | copy-done | bytes 49176
  2.9 0.0 copy-start.3
  2.9 0.7 %copy-done.3 = bf16[1,3072]{1,0:T(2,128)(2,1)S(1)} copy-done((bf16[1,3072]{1,0:T(2,128)(2,1)S(1)}, bf16[1,3072]{1,0:T(2,128)(2,1)}, u32[]{:S(2)}) %copy-start.3) | copy-done | bytes 6168
  3.6 0.0 copy-start.4
  3.6 0.7 %copy-done.4 = bf16[1,512]{1,0:T(2,128)(2,1)S(1)} copy-done((bf16[1,512]{1,0:T(2,128)(2,1)S(1)}, bf16[1,512]{1,0:T(2,128)(2,1)}, u32[]{:S(2)}) %copy-start.4) | copy-done | bytes 1048
  4.3 0.0 copy-start.5
  4.3 0.7 %copy-done.5 = bf16[1,512]{1,0:T(2,128)(2,1)S(1)} copy-done((bf16[1,512]{1,0:T(2,128)(2,1)S(1)}, bf16[1,512]{1,0:T(2,128)(2,1)}, u32[]{:S(2)}) %copy-start.5) | copy-done | bytes 1048
  5.0 0.0 copy-start.6
  5.0 0.7 %copy-done.6 = s32[4]{0:T(128)S(1)} copy-done((s32[4]{0:T(128)S(1)}, s32[4]{0:T(128)}, u32[]{:S(2)}) %copy-start.6) | copy-done | bytes 40
  5.6 1.2 %attend.1 = bf16[32,24,128]{2,1,0:T(8,128)(2,1)S(1)} custom-call(s32[4]{0:T(128)S(1)} %copy-done.6, bf16[1,3072]{1,0:T(2,128)(2,1)S(1)} %copy-done.3, bf16[1,512,512]{2,1,0:T(8,128)(2,1)S(1)} %copy-done, bf16[1,512,512]{2,1,0:T(8,128)(2,1)S(1)} %copy-done.1, bf16[1,512]{1,0:T(2,128)(2,1)S(1)} %copy-done.4, bf16[1,512]{1,0:T(2,128)(2,1)S(1)} %copy-done.5, ...), custom_call_target="tpu_custom_call" | custom-call | tf_op jit(solution)/shard_map/attend/pallas_call | solution.py:81
  6.8 16.3 %all_to_all.10.parts = bf16[32,24,128]{2,1,0:T(8,128)(2,1)} all-to-all(bf16[32,24,128]{2,1,0:T(8,128)(2,1)S(1)} %attend.1), channel_id=1, replica_groups=mesh['grp'=4,'dev'=8] {'grp','dev'}, dimensions={0} | all-to-all | bytes 393216 | tf_op jit(solution)/shard_map/all_to_all | solution.py:265
  23.1 0.0 copy-start.7
  23.1 0.0 copy-start.8
  23.1 28.9 %experts.1 = bf16[32,4,768]{2,1,0:T(4,128)(2,1)} custom-call(bf16[32,24,128]{2,1,0:T(8,128)(2,1)} %all_to_all.10.parts, f32[48,128]{1,0:T(8,128)} %bitcast.1, bf16[6144,2048]{1,0:T(8,128)(2,1)} %w_gate.1, bf16[6144,2048]{1,0:T(8,128)(2,1)} %w_up.1, bf16[2048,6144]{1,0:T(8,128)(2,1)} %w_down.1), custom_call_target="tpu_custom_call" | custom-call | tf_op jit(solution)/shard_map/experts/pallas_call | solution.py:178
  52.0 2.3 %all-to-all-start.1 = ((bf16[32,4,768]{2,1,0:T(4,128)(2,1)}), bf16[32,4,768]{2,1,0:T(4,128)(2,1)S(1)}, u32[]{:S(2)}, u32[]{:S(2)}) async-start(bf16[32,4,768]{2,1,0:T(4,128)(2,1)} %experts.1), calls=%async_computation.1 | async-start | bytes 393216 | tf_op jit(solution)/shard_map/all_to_all | solution.py:268
  54.3 0.0 copy-done.7
  54.3 0.1 copy.14.ids
  54.4 0.0 copy-done.8
  54.4 0.1 copy.15.logits
  54.5 8.9 %all-to-all-done.1.parts = bf16[32,4,768]{2,1,0:T(4,128)(2,1)S(1)} async-done(((bf16[32,4,768]{2,1,0:T(4,128)(2,1)}), bf16[32,4,768]{2,1,0:T(4,128)(2,1)S(1)}, u32[]{:S(2)}, u32[]{:S(2)}) %all-to-all-start.1) | async-done | bytes 196640 | tf_op jit(solution)/shard_map/all_to_all | solution.py:268
  63.4 0.9 %combine.1 = bf16[4,768]{1,0:T(4,128)(2,1)} custom-call(bf16[32,4,768]{2,1,0:T(4,128)(2,1)S(1)} %all-to-all-done.1.parts, s32[4,2]{1,0:T(4,128)S(1)} %copy.14.ids, f32[4,2]{1,0:T(4,128)S(1)} %copy.15.logits), custom_call_target="tpu_custom_call" | custom-call | tf_op jit(solution)/shard_map/combine/pallas_call | solution.py:233
Async XLA Ops:
  0.0 1.0 %copy-start = (bf16[1,512,512]{2,1,0:T(8,128)(2,1)S(1)}, bf16[1,512,512]{2,1,0:T(8,128)(2,1)}, u32[]{:S(2)}) copy-start(bf16[1,512,512]{2,1,0:T(8,128)(2,1)} %key_rows.1) | copy-start | bytes 1572868
  1.0 1.0 %copy-start.1 = (bf16[1,512,512]{2,1,0:T(8,128)(2,1)S(1)}, bf16[1,512,512]{2,1,0:T(8,128)(2,1)}, u32[]{:S(2)}) copy-start(bf16[1,512,512]{2,1,0:T(8,128)(2,1)} %value_rows.1) | copy-start | bytes 1572868
  2.1 0.8 %copy-start.2 = (bf16[4,6144]{1,0:T(4,128)(2,1)S(1)}, bf16[4,6144]{1,0:T(4,128)(2,1)}, u32[]{:S(2)}) copy-start(bf16[4,6144]{1,0:T(4,128)(2,1)} %residual.1) | copy-start | bytes 147460
  2.9 0.7 %copy-start.3 = (bf16[1,3072]{1,0:T(2,128)(2,1)S(1)}, bf16[1,3072]{1,0:T(2,128)(2,1)}, u32[]{:S(2)}) copy-start(bf16[1,3072]{1,0:T(2,128)(2,1)} %queries.1) | copy-start | bytes 18436
  3.6 0.7 %copy-start.4 = (bf16[1,512]{1,0:T(2,128)(2,1)S(1)}, bf16[1,512]{1,0:T(2,128)(2,1)}, u32[]{:S(2)}) copy-start(bf16[1,512]{1,0:T(2,128)(2,1)} %new_keys.1) | copy-start | bytes 3076
  4.3 0.7 %copy-start.5 = (bf16[1,512]{1,0:T(2,128)(2,1)S(1)}, bf16[1,512]{1,0:T(2,128)(2,1)}, u32[]{:S(2)}) copy-start(bf16[1,512]{1,0:T(2,128)(2,1)} %new_values.1) | copy-start | bytes 3076
  5.0 0.7 %copy-start.6 = (s32[4]{0:T(128)S(1)}, s32[4]{0:T(128)}, u32[]{:S(2)}) copy-start(s32[4]{0:T(128)} %lengths.1) | copy-start | bytes 52
  23.1 31.2 %copy-start.7 = (s32[4,2]{0,1:T(2,128)S(1)}, s32[4,2]{0,1:T(2,128)}, u32[]{:S(2)}) copy-start(s32[4,2]{0,1:T(2,128)} %param.21) | copy-start | bytes 100
  23.1 31.3 %copy-start.8 = (f32[4,2]{0,1:T(2,128)S(1)}, f32[4,2]{0,1:T(2,128)}, u32[]{:S(2)}) copy-start(f32[4,2]{0,1:T(2,128)} %param.22) | copy-start | bytes 100
  52.0 11.5 %all-to-all-start.1 = ((bf16[32,4,768]{2,1,0:T(4,128)(2,1)}), bf16[32,4,768]{2,1,0:T(4,128)(2,1)S(1)}, u32[]{:S(2)}, u32[]{:S(2)}) async-start(bf16[32,4,768]{2,1,0:T(4,128)(2,1)} %experts.1), calls=%async_computation.1 | async-start | bytes 393216 | tf_op jit(solution)/shard_map/all_to_all | solution.py:268

commit v2 on v1

v2 whole, which is shorter than its diff:
```python
import functools

import jax
import jax.numpy as jnp
from jax import lax
from jax.experimental import pallas as pl
from jax.experimental.pallas import tpu as pltpu
from jax.sharding import PartitionSpec as P

QUERY_HEADS = 48
KEY_VALUE_HEADS = 8
HEAD_SIZE = 128
E = 8
SHARING_DEVICES = 2
GROUP_WIDTH = QUERY_HEADS // KEY_VALUE_HEADS
LOCAL_HEADS = QUERY_HEADS // SHARING_DEVICES
MIB = 2**20
VMEM = pl.BlockSpec(memory_space=pltpu.VMEM)
HBM = pl.BlockSpec(memory_space=pltpu.HBM)
TILE = 512
EARLY_TILES = 0
HALF_TILE = 256
POOL = 9


def in_hbm(*arrays):
    return [pltpu.with_memory_space_constraint(a, pltpu.HBM) for a in arrays]


def in_vmem(*arrays):
    return [pltpu.with_memory_space_constraint(a, pltpu.VMEM) for a in arrays]


def head_rows(row):
    heads = row.shape[1] // HEAD_SIZE
    return jnp.concatenate(
        [row[:, j * HEAD_SIZE : (j + 1) * HEAD_SIZE] for j in range(heads)], axis=0
    )


def tile_source(w_gate, w_up, n):
    return (w_gate, w_up)[n % 2].at[:, pl.ds(n // 2 * TILE, TILE)]


def attend_kernel(early, *refs):
    lengths, queries, key_rows, value_rows, new_keys, new_values, residual = refs[:7]
    out = refs[7 + 2 * (early > 0)]
    buffers = refs[-9:-1]
    length_buf, query_buf, key_buf, value_buf, new_key_buf, new_value_buf, residual_buf = buffers[:7]
    sems, tile_sems = buffers[7], refs[-1]
    sequence, half = lax.axis_index("pair"), lax.axis_index("half")
    heads = LOCAL_HEADS
    columns = heads * HEAD_SIZE
    at = pl.ds(pl.multiple_of(half * columns, HEAD_SIZE), columns)
    pairs = [
        (key_rows.at[0], key_buf),
        (queries, query_buf),
        (new_keys, new_key_buf),
        (lengths, length_buf),
        (new_values, new_value_buf),
        (value_rows.at[0], value_buf),
        (residual.at[:, at], residual_buf),
    ]
    copies = [pltpu.make_async_copy(*pair, sems.at[i]) for i, pair in enumerate(pairs)]
    if early:
        w_gate, w_up, tiles = refs[7], refs[8], refs[10]
        tile_copies = [
            pltpu.make_async_copy(tile_source(w_gate, w_up, n), tiles.at[n], tile_sems.at[n])
            for n in range(early)
        ]
    else:
        tile_copies = []
    for copy in copies + tile_copies:
        copy.start()
    cache_len, width = key_buf.shape
    kv_heads = width // HEAD_SIZE
    scale = HEAD_SIZE ** (-0.5)
    for copy in copies[:4]:
        copy.wait()
    query = head_rows(query_buf[...].astype(jnp.float32))
    owner = lax.broadcasted_iota(jnp.int32, (heads, HEAD_SIZE), 0) // GROUP_WIDTH
    blocks = [jnp.where(owner == b, query, 0.0) for b in range(kv_heads)]
    spread = jnp.concatenate(blocks, axis=1)
    scores = (
        lax.dot_general(
            spread.astype(jnp.bfloat16),
            key_buf[...],
            (((1,), (1,)), ((), ())),
            preferred_element_type=jnp.float32,
        )
        * scale
    )
    places = lax.broadcasted_iota(jnp.int32, (heads, cache_len), 1)
    scores = jnp.where(places < length_buf[sequence], scores, -1e30)
    new_score = (
        jnp.sum(spread * new_key_buf[...].astype(jnp.float32), axis=1, keepdims=True) * scale
    )
    row_max = jnp.maximum(jnp.max(scores, axis=1, keepdims=True), new_score)
    exp_all = jnp.exp(scores - row_max)
    exp_new = jnp.exp(new_score - row_max)
    denom = jnp.sum(exp_all, axis=1, keepdims=True) + exp_new
    weights = (exp_all / denom).astype(jnp.bfloat16)
    weight_new = (exp_new / denom).astype(jnp.bfloat16).astype(jnp.float32)
    for copy in copies[4:]:
        copy.wait()
    mixed = jnp.dot(weights, value_buf[...], preferred_element_type=jnp.float32)
    mixed = mixed + weight_new * new_value_buf[...].astype(jnp.float32)
    attended = jnp.zeros((heads, HEAD_SIZE), jnp.float32)
    for b in range(kv_heads):
        attended = jnp.where(
            owner == b, mixed[:, b * HEAD_SIZE : (b + 1) * HEAD_SIZE], attended
        )
    attended = attended.astype(jnp.bfloat16).astype(jnp.float32)
    mine = residual_buf[...].astype(jnp.float32)
    rows = lax.broadcasted_iota(jnp.int32, mine.shape, 0)
    mine = jnp.sum(jnp.where(rows == sequence, mine, 0.0), axis=0, keepdims=True)
    out[...] = attended + head_rows(mine)
    for copy in tile_copies:
        copy.wait()


def attend(lengths, queries, key_rows, value_rows, new_keys, new_values, residual, w_gate, w_up, early):
    half_columns = LOCAL_HEADS * HEAD_SIZE
    out_shape = [jax.ShapeDtypeStruct((LOCAL_HEADS, HEAD_SIZE), jnp.float32)]
    operands = [lengths, queries, key_rows, value_rows, new_keys, new_values, residual]
    if early:
        out_shape.append(pltpu.VMEM((early, w_gate.shape[0], TILE), jnp.bfloat16))
        operands += [w_gate, w_up]
    return pl.pallas_call(
        functools.partial(attend_kernel, early),
        out_shape=out_shape,
        in_specs=[HBM] * len(operands),
        out_specs=[VMEM] * len(out_shape),
        scratch_shapes=[
            pltpu.SMEM(lengths.shape, jnp.int32),
            pltpu.VMEM(queries.shape, jnp.bfloat16),
            pltpu.VMEM(key_rows.shape[1:], jnp.bfloat16),
            pltpu.VMEM(value_rows.shape[1:], jnp.bfloat16),
            pltpu.VMEM(new_keys.shape, jnp.bfloat16),
            pltpu.VMEM(new_values.shape, jnp.bfloat16),
            pltpu.VMEM((residual.shape[0], half_columns), jnp.bfloat16),
            pltpu.SemaphoreType.DMA((7,)),
            pltpu.SemaphoreType.DMA((max(early, 1),)),
        ],
        compiler_params=pltpu.CompilerParams(vmem_limit_bytes=8 * MIB),
        name="attend",
    )(*in_hbm(*operands))


def norm_kernel(mine, other, gain, out):
    first = lax.axis_index("half") == 0
    row = jnp.concatenate(
        [jnp.where(first, mine[...], other[...]), jnp.where(first, other[...], mine[...])], axis=0
    )
    square = jnp.sum(jnp.sum(row * row, axis=0, keepdims=True), axis=1, keepdims=True)
    inverse = lax.rsqrt(square * (1.0 / (row.shape[0] * HEAD_SIZE)) + 1e-05)
    normed = (row * inverse * gain[...]).astype(jnp.bfloat16)
    out[...] = jnp.broadcast_to(normed[None], out.shape)


def norm(mine, other, gain, chips):
    heads = gain.shape[0] // HEAD_SIZE
    return pl.pallas_call(
        norm_kernel,
        out_shape=jax.ShapeDtypeStruct((chips, heads, HEAD_SIZE), jnp.bfloat16),
        in_specs=[VMEM] * 3,
        out_specs=VMEM,
        compiler_params=pltpu.CompilerParams(vmem_limit_bytes=16 * MIB),
        name="norm",
    )(mine, other, gain.reshape(heads, HEAD_SIZE))


def experts_kernel(
    parts, w_gate, w_up, w_down, out, flat, normed, hidden, pool, sems
):
    tokens, width = normed.shape
    local_hidden = w_down.shape[0]
    tiles = 2 * (local_hidden // TILE)
    held = []
    first = len(held)
    per_slot = width // local_hidden
    slots, heads = pool.shape[0], width // HEAD_SIZE
    group_rows, columns = out.shape[1:]
    targets = width // columns

    blocks = width // TILE
    items = [("tile", n) for n in range(first, tiles)]
    items += [("down", n) for n in range(0, blocks, per_slot)]

    def copies(i):
        kind, n = items[i]
        slot = i % slots
        if kind == "tile":
            return [pltpu.make_async_copy(tile_source(w_gate, w_up, n), pool.at[slot], sems.at[slot, 0])]
        return [
            pltpu.make_async_copy(
                w_down.at[:, pl.ds((n + k) * TILE, TILE)],
                pool.at[slot, pl.ds(k * local_hidden, local_hidden), :],
                sems.at[slot, k],
            )
            for k in range(per_slot)
        ]

    def begin(i):
        if i < len(items):
            for copy in copies(i):
                copy.start()

    for i in range(slots):
        begin(i)

    flat[...] = parts[...].astype(jnp.float32).reshape(flat.shape)
    for j in range(heads):
        normed[:, j * HEAD_SIZE : (j + 1) * HEAD_SIZE] = flat[
            pl.ds(j, tokens, stride=heads), :
        ].astype(jnp.bfloat16)

    for n in range(tiles):
        if n < first:
            weight = held[n][...]
        else:
            copies(n - first)[0].wait()
            weight = pool[(n - first) % slots]
        product = jnp.dot(normed[...], weight, preferred_element_type=jnp.float32)
        if n >= first:
            begin(n - first + slots)
        if n % 2 == 0:
            gate = product
        else:
            at = slice(n // 2 * TILE, (n // 2 + 1) * TILE)
            hidden[:, at] = (gate / (1.0 + jnp.exp(-gate)) * product).astype(jnp.bfloat16)

    step = HALF_TILE
    for i in range(tiles - first, len(items)):
        for k, copy in enumerate(copies(i)):
            copy.wait()
            weight = pool[i % slots, k * local_hidden : (k + 1) * local_hidden, :]
            part = jnp.dot(hidden[...], weight, preferred_element_type=jnp.float32)
            block = items[i][1] + k
            for q in range(TILE // step):
                target, column = divmod(block * TILE + q * step, columns)
                for g in range(tokens // group_rows):
                    out[g * targets + target, :, column : column + step] = part[
                        g * group_rows : (g + 1) * group_rows, q * step : (q + 1) * step
                    ].astype(out.dtype)
        begin(i + slots)


def experts(parts, w_gate, w_up, w_down, group_rows, dev_count):
    tokens = parts.shape[0]
    width, local_hidden = w_gate.shape
    columns = width // dev_count
    return pl.pallas_call(
        experts_kernel,
        out_shape=jax.ShapeDtypeStruct((SHARING_DEVICES * tokens, group_rows, columns), jnp.bfloat16),
        in_specs=[VMEM, HBM, HBM, HBM],
        out_specs=VMEM,
        scratch_shapes=[
            pltpu.VMEM((tokens * width // HEAD_SIZE, HEAD_SIZE), jnp.float32),
            pltpu.VMEM((tokens, width), jnp.bfloat16),
            pltpu.VMEM((tokens, local_hidden), jnp.bfloat16),
            pltpu.VMEM((POOL, width, TILE), jnp.bfloat16),
            pltpu.SemaphoreType.DMA((POOL, width // local_hidden)),
        ],
        compiler_params=pltpu.CompilerParams(vmem_limit_bytes=(6 * POOL + 2) * MIB),
        name="experts",
    )(*in_vmem(parts), *in_hbm(w_gate, w_up, w_down))


def experts_plain(parts, w_gate, w_up, w_down, group_rows, dev_count):
    width = w_gate.shape[0]
    normed = parts.reshape(-1, width)
    gate = jnp.dot(normed, w_gate, preferred_element_type=jnp.float32)
    up = jnp.dot(normed, w_up, preferred_element_type=jnp.float32)
    hidden = (jax.nn.silu(gate) * up).astype(jnp.bfloat16)
    part = jnp.dot(hidden, w_down, preferred_element_type=jnp.float32).astype(jnp.bfloat16)
    part = part.reshape(-1, group_rows, dev_count, width // dev_count)
    return part.transpose(0, 2, 1, 3).reshape(-1, group_rows, width // dev_count)


def combine_kernel(per_expert, dev_count, parts, ids, logits, out):
    shards = parts.shape[0] // dev_count
    logit = logits[...]
    top = jnp.max(logit, axis=1, keepdims=True)
    raised = jnp.exp(logit - top)
    probs = raised / jnp.sum(raised, axis=1, keepdims=True)
    chosen = ids[...]
    total = jnp.zeros(out.shape, jnp.float32)
    for e in range(E):
        weight = jnp.sum(jnp.where(chosen == e, probs, 0.0), axis=1, keepdims=True)
        here = jnp.zeros(out.shape, jnp.float32)
        for g in range(shards):
            for c in range(per_expert):
                here = here + parts[g * dev_count + e * per_expert + c].astype(jnp.float32)
        total = total + weight * here
    out[...] = total.astype(out.dtype)


def combine(parts, ids, logits, dev_count):
    return pl.pallas_call(
        functools.partial(combine_kernel, dev_count // E, dev_count),
        out_shape=jax.ShapeDtypeStruct(parts.shape[1:], jnp.bfloat16),
        in_specs=[VMEM] * 3,
        out_specs=VMEM,
        compiler_params=pltpu.CompilerParams(vmem_limit_bytes=24 * MIB),
        name="combine",
    )(parts, ids, logits)


def body(
    queries,
    cached_key_rows,
    cached_value_rows,
    incoming_keys,
    incoming_values,
    lengths,
    residual,
    norm_gain,
    expert_ids,
    route_logits,
    w_gate,
    w_up,
    w_down,
):
    chips = lax.axis_size("grp") * lax.axis_size("pair")
    dev_count = lax.axis_size("pair") * SHARING_DEVICES
    group_rows = residual.shape[0]
    streamed = w_gate.shape[1] == 4 * TILE
    summed, *early = attend(
        lengths, queries, cached_key_rows, cached_value_rows, incoming_keys, incoming_values,
        residual, w_gate, w_up, EARLY_TILES if streamed else 0,
    )
    other = lax.ppermute(summed, "half", [(0, 1), (1, 0)])
    sent = norm(summed, other, norm_gain, chips)
    rows = lax.all_to_all(sent, ("grp", "pair"), 0, 0, tiled=True)
    if streamed:
        part = experts(rows, *early, w_gate, w_up, w_down, group_rows, dev_count)
    else:
        part = experts_plain(rows, w_gate, w_up, w_down, group_rows, dev_count)
    got = lax.all_to_all(part, ("grp", "pair", "half"), 0, 0, tiled=True)
    return combine(got, expert_ids, route_logits, dev_count)


def solution(mesh):
    groups, dev_count = mesh.devices.shape
    split = jax.sharding.Mesh(
        mesh.devices.reshape(groups, dev_count // SHARING_DEVICES, SHARING_DEVICES),
        ("grp", "pair", "half"),
    )
    dev = ("pair", "half")
    rows = ("grp",) + dev
    shards = dev + ("grp",)
    return jax.shard_map(
        body,
        mesh=split,
        in_specs=(
            P(rows, None),
            P(rows, None, None),
            P(rows, None, None),
            P(rows, None),
            P(rows, None),
            P("grp"),
            P("grp", None),
            P(),
            P("grp", None),
            P("grp", None),
            P(None, shards),
            P(None, shards),
            P(shards, None),
        ),
        out_specs=P("grp", dev),
        check_vma=False,
    )
```

time: 64.7 us -> 58.7 us (0.907)
  local copies, waits for them, and re-layouts: 5.8 us -> 0.93 us
  Pallas kernels: 30.9 us -> 27.1 us
  starting transfers between devices: 2.34 us -> 5.47 us
  blocking collectives: 16.3 us -> 14.5 us
  waiting for transfers between devices: 8.94 us -> 10.4 us
    unnamed x20 -> x8, local copies, waits for them, and re-layouts: 5.8 us -> 0.93 us
    pallas_call x2 -> x3, Pallas kernels: 30 us -> 26.3 us  [the longest x1 24.4 us: experts(): pl.pallas_call(experts_kernel, out_shape=jax.ShapeDtypeStruct((SHARING_DE...]
    all_to_all x1, starting transfers between devices: 2.34 us -> 5.35 us  [body(): got = lax.all_to_all(part, ('grp', 'pair', 'half'), 0, 0, tiled=True)]
    all_to_all x1, blocking collectives: 16.3 us -> 14.5 us  [body(): rows = lax.all_to_all(sent, ('grp', 'pair'), 0, 0, tiled=True)]
    ppermute x0 -> x1, waiting for transfers between devices: none -> 1.12 us  [body(): other = lax.ppermute(summed, 'half', [(0, 1), (1, 0)])]
  transfers between devices with their start and end apart: 1 -> 2, of which waited for: 1 -> 2; matrix products, arithmetic and copies ran while one was open for 0% -> 0% of each run, Pallas kernels for 0% -> 0%
where the time goes in v2:
time: 58.7 us; the launch traced here: 58.4 us
  Pallas kernels  27.1 us (46%)
  blocking collectives  14.5 us (25%)
  waiting for transfers between devices  10.4 us (18%)
  starting transfers between devices  5.47 us (9%)
  local copies, waits for them, and re-layouts  0.93 us (2%)
    pallas_call x1, Pallas kernels, experts(): pl.pallas_call(experts_kernel, out_shape=jax.ShapeDtypeStruct((SHARING_DE...  24.4 us
    all_to_all x1, blocking collectives, body(): rows = lax.all_to_all(sent, ('grp', 'pair'), 0, 0, tiled=True)  14.5 us
    all_to_all x1, waiting for transfers between devices, body(): got = lax.all_to_all(part, ('grp', 'pair', 'half'), 0, 0, tiled=True)  9.23 us
    all_to_all x1, starting transfers between devices, body(): got = lax.all_to_all(part, ('grp', 'pair', 'half'), 0, 0, tiled=True)  5.35 us
    pallas_call x1, Pallas kernels, attend(): pl.pallas_call(functools.partial(attend_kernel, early), out_shape=out_sha...  1.77 us
  transfers between devices with their start and end apart: 2, of which 2 were waited for; matrix products, arithmetic and copies ran while one was open for 0% of the time, Pallas kernels for 0%

profile of v2, /device:TPU:1, one launch (start us, length us, event | category | flops | bytes accessed | tf_op | source)
XLA Modules:
  0.0 58.4 jit_solution(2823651313809395510)
XLA Ops:
  0.0 1.8 %attend.1.mine = f32[24,128]{1,0:T(8,128)S(1)} custom-call(s32[4]{0:T(128)} %refs_0_.1, bf16[1,3072]{1,0:T(2,128)(2,1)} %refs_1_.1, bf16[1,512,512]{2,1,0:T(8,128)(2,1)} %refs_2_.1, bf16[1,512,512]{2,1,0:T(8,128)(2,1)} %refs_3_.1, bf16[1,512]{1,0:T(2,128)(2,1)} %refs_4_.1, bf16[1,512]{1,0:T(2,128)(2,1)} %refs_5_.1, bf16[4,6144]{1,0:T(4,128)(2,1)} %refs_6_.1), custom_call_target="tpu_custom_call" | custom-call | tf_op jit(solution)/shard_map/attend/pallas_call | solution.py:129
  1.8 0.1 collective-permute-start
  1.9 1.1 %collective-permute-done.other = f32[24,128]{1,0:T(8,128)S(1)} collective-permute-done((f32[24,128]{1,0:T(8,128)S(1)}, f32[24,128]{1,0:T(8,128)S(1)}, u32[]{:S(2)}, u32[]{:S(2)}) %collective-permute-start) | collective-permute-done | bytes 12320 | tf_op jit(solution)/shard_map/ppermute | solution.py:333
  3.0 0.0 copy-start
  3.0 0.7 %copy-done = f32[6144]{0:T(1024)S(1)} copy-done((f32[6144]{0:T(1024)S(1)}, f32[6144]{0:T(1024)}, u32[]{:S(2)}) %copy-start) | copy-done | bytes 24600
  3.8 0.1 norm.1
  3.9 14.5 %all_to_all.10.parts = bf16[16,48,128]{2,1,0:T(8,128)(2,1)S(1)} all-to-all(bf16[16,48,128]{2,1,0:T(8,128)(2,1)S(1)} %norm.1), channel_id=1, replica_groups=mesh['grp'=4,'pair'=4,'half'=2] {'grp','pair'}, dimensions={0} | all-to-all | bytes 393216 | tf_op jit(solution)/shard_map/all_to_all | solution.py:335
  18.4 0.0 copy-start.1
  18.4 0.0 copy-start.2
  18.4 24.4 %experts.1 = bf16[32,4,768]{2,1,0:T(4,128)(2,1)} custom-call(bf16[16,48,128]{2,1,0:T(8,128)(2,1)S(1)} %all_to_all.10.parts, bf16[6144,2048]{1,0:T(8,128)(2,1)} %w_gate.1, bf16[6144,2048]{1,0:T(8,128)(2,1)} %w_up.1, bf16[2048,6144]{1,0:T(8,128)(2,1)} %w_down.1), custom_call_target="tpu_custom_call" | custom-call | tf_op jit(solution)/shard_map/experts/pallas_call | solution.py:253
  42.8 5.3 %all-to-all-start.1 = ((bf16[32,4,768]{2,1,0:T(4,128)(2,1)}), bf16[32,4,768]{2,1,0:T(4,128)(2,1)S(1)}, u32[]{:S(2)}, u32[]{:S(2)}) async-start(bf16[32,4,768]{2,1,0:T(4,128)(2,1)} %experts.1), calls=%async_computation.1 | async-start | bytes 393216 | tf_op jit(solution)/shard_map/all_to_all | solution.py:340
  48.1 0.0 copy-done.1
  48.2 0.1 copy.14.ids
  48.3 0.0 copy-done.2
  48.3 0.1 copy.15.logits
  48.3 9.2 %all-to-all-done.1.parts = bf16[32,4,768]{2,1,0:T(4,128)(2,1)S(1)} async-done(((bf16[32,4,768]{2,1,0:T(4,128)(2,1)}), bf16[32,4,768]{2,1,0:T(4,128)(2,1)S(1)}, u32[]{:S(2)}, u32[]{:S(2)}) %all-to-all-start.1) | async-done | bytes 196640 | tf_op jit(solution)/shard_map/all_to_all | solution.py:340
  57.6 0.9 %combine.1 = bf16[4,768]{1,0:T(4,128)(2,1)} custom-call(bf16[32,4,768]{2,1,0:T(4,128)(2,1)S(1)} %all-to-all-done.1.parts, s32[4,2]{1,0:T(4,128)S(1)} %copy.14.ids, f32[4,2]{1,0:T(4,128)S(1)} %copy.15.logits), custom_call_target="tpu_custom_call" | custom-call | tf_op jit(solution)/shard_map/combine/pallas_call | solution.py:300
Async XLA Ops:
  1.8 1.2 %collective-permute-start = (f32[24,128]{1,0:T(8,128)S(1)}, f32[24,128]{1,0:T(8,128)S(1)}, u32[]{:S(2)}, u32[]{:S(2)}) collective-permute-start(f32[24,128]{1,0:T(8,128)S(1)} %attend.1.mine), channel_id=1, source_target_pairs={{0,1},{1,0},{2,3},{3,2},{4,5},{5,4},{6,7},{7,6},{8,9},{9,8},{10,11... | collective-permute-start | bytes 36872 | tf_op jit(solution)/shard_map/ppermute | solution.py:333
  3.0 0.7 %copy-start = (f32[6144]{0:T(1024)S(1)}, f32[6144]{0:T(1024)}, u32[]{:S(2)}) copy-start(f32[6144]{0:T(1024)} %param.20) | copy-start | bytes 73732
  18.4 29.7 %copy-start.1 = (s32[4,2]{0,1:T(2,128)S(1)}, s32[4,2]{0,1:T(2,128)}, u32[]{:S(2)}) copy-start(s32[4,2]{0,1:T(2,128)} %param.21) | copy-start | bytes 100
  18.4 29.8 %copy-start.2 = (f32[4,2]{0,1:T(2,128)S(1)}, f32[4,2]{0,1:T(2,128)}, u32[]{:S(2)}) copy-start(f32[4,2]{0,1:T(2,128)} %param.22) | copy-start | bytes 100
  42.8 14.8 %all-to-all-start.1 = ((bf16[32,4,768]{2,1,0:T(4,128)(2,1)}), bf16[32,4,768]{2,1,0:T(4,128)(2,1)S(1)}, u32[]{:S(2)}, u32[]{:S(2)}) async-start(bf16[32,4,768]{2,1,0:T(4,128)(2,1)} %experts.1), calls=%async_computation.1 | async-start | bytes 393216 | tf_op jit(solution)/shard_map/all_to_all | solution.py:340

commit v3 on v2

--- a/solution.py
+++ b/solution.py
@@ -18,9 +18,9 @@
 VMEM = pl.BlockSpec(memory_space=pltpu.VMEM)
 HBM = pl.BlockSpec(memory_space=pltpu.HBM)
 TILE = 512
-EARLY_TILES = 0
-HALF_TILE = 256
-POOL = 9
+PART = 256
+RING = 6
+UNTIL_ROWS = pl.CostEstimate(flops=40_000_000_000, bytes_accessed=0, transcendentals=0)
 
 
 def in_hbm(*arrays):
@@ -38,16 +38,10 @@
     )
 
 
-def tile_source(w_gate, w_up, n):
-    return (w_gate, w_up)[n % 2].at[:, pl.ds(n // 2 * TILE, TILE)]
-
-
-def attend_kernel(early, *refs):
-    lengths, queries, key_rows, value_rows, new_keys, new_values, residual = refs[:7]
-    out = refs[7 + 2 * (early > 0)]
-    buffers = refs[-9:-1]
-    length_buf, query_buf, key_buf, value_buf, new_key_buf, new_value_buf, residual_buf = buffers[:7]
-    sems, tile_sems = buffers[7], refs[-1]
+def attend_kernel(
+    lengths, queries, key_rows, value_rows, new_keys, new_values, residual, out,
+    length_buf, query_buf, key_buf, value_buf, new_key_buf, new_value_buf, residual_buf, sems,
+):
     sequence, half = lax.axis_index("pair"), lax.axis_index("half")
     heads = LOCAL_HEADS
     columns = heads * HEAD_SIZE
@@ -62,15 +56,7 @@
         (residual.at[:, at], residual_buf),
     ]
     copies = [pltpu.make_async_copy(*pair, sems.at[i]) for i, pair in enumerate(pairs)]
-    if early:
-        w_gate, w_up, tiles = refs[7], refs[8], refs[10]
-        tile_copies = [
-            pltpu.make_async_copy(tile_source(w_gate, w_up, n), tiles.at[n], tile_sems.at[n])
-            for n in range(early)
-        ]
-    else:
-        tile_copies = []
-    for copy in copies + tile_copies:
+    for copy in copies:
         copy.start()
     cache_len, width = key_buf.shape
     kv_heads = width // HEAD_SIZE
@@ -115,22 +101,16 @@
     rows = lax.broadcasted_iota(jnp.int32, mine.shape, 0)
     mine = jnp.sum(jnp.where(rows == sequence, mine, 0.0), axis=0, keepdims=True)
     out[...] = attended + head_rows(mine)
-    for copy in tile_copies:
-        copy.wait()
-
-
-def attend(lengths, queries, key_rows, value_rows, new_keys, new_values, residual, w_gate, w_up, early):
+
+
+def attend(lengths, queries, key_rows, value_rows, new_keys, new_values, residual):
     half_columns = LOCAL_HEADS * HEAD_SIZE
-    out_shape = [jax.ShapeDtypeStruct((LOCAL_HEADS, HEAD_SIZE), jnp.float32)]
     operands = [lengths, queries, key_rows, value_rows, new_keys, new_values, residual]
-    if early:
-        out_shape.append(pltpu.VMEM((early, w_gate.shape[0], TILE), jnp.bfloat16))
-        operands += [w_gate, w_up]
     return pl.pallas_call(
-        functools.partial(attend_kernel, early),
-        out_shape=out_shape,
+        attend_kernel,
+        out_shape=jax.ShapeDtypeStruct((LOCAL_HEADS, HEAD_SIZE), jnp.float32),
         in_specs=[HBM] * len(operands),
-        out_specs=[VMEM] * len(out_shape),
+        out_specs=VMEM,
         scratch_shapes=[
             pltpu.SMEM(lengths.shape, jnp.int32),
             pltpu.VMEM(queries.shape, jnp.bfloat16),
@@ -140,9 +120,9 @@
             pltpu.VMEM(new_values.shape, jnp.bfloat16),
             pltpu.VMEM((residual.shape[0], half_columns), jnp.bfloat16),
             pltpu.SemaphoreType.DMA((7,)),
-            pltpu.SemaphoreType.DMA((max(early, 1),)),
         ],
-        compiler_params=pltpu.CompilerParams(vmem_limit_bytes=8 * MIB),
+        compiler_params=pltpu.CompilerParams(vmem_limit_bytes=4 * MIB),
+        cost_estimate=UNTIL_ROWS,
         name="attend",
     )(*in_hbm(*operands))
 
@@ -165,49 +145,25 @@
         out_shape=jax.ShapeDtypeStruct((chips, heads, HEAD_SIZE), jnp.bfloat16),
         in_specs=[VMEM] * 3,
         out_specs=VMEM,
-        compiler_params=pltpu.CompilerParams(vmem_limit_bytes=16 * MIB),
+        compiler_params=pltpu.CompilerParams(vmem_limit_bytes=MIB + 4 * chips * gain.shape[0]),
         name="norm",
     )(mine, other, gain.reshape(heads, HEAD_SIZE))
 
 
-def experts_kernel(
-    parts, w_gate, w_up, w_down, out, flat, normed, hidden, pool, sems
-):
+def experts_kernel(parts, w_gate, w_up, w_down, out, flat, normed, hidden, ring, sems):
     tokens, width = normed.shape
     local_hidden = w_down.shape[0]
-    tiles = 2 * (local_hidden // TILE)
-    held = []
-    first = len(held)
-    per_slot = width // local_hidden
-    slots, heads = pool.shape[0], width // HEAD_SIZE
+    slots, heads = ring.shape[0], width // HEAD_SIZE
     group_rows, columns = out.shape[1:]
     targets = width // columns
-
     blocks = width // TILE
-    items = [("tile", n) for n in range(first, tiles)]
-    items += [("down", n) for n in range(0, blocks, per_slot)]
-
-    def copies(i):
-        kind, n = items[i]
-        slot = i % slots
-        if kind == "tile":
-            return [pltpu.make_async_copy(tile_source(w_gate, w_up, n), pool.at[slot], sems.at[slot, 0])]
-        return [
-            pltpu.make_async_copy(
-                w_down.at[:, pl.ds((n + k) * TILE, TILE)],
-                pool.at[slot, pl.ds(k * local_hidden, local_hidden), :],
-                sems.at[slot, k],
-            )
-            for k in range(per_slot)
-        ]
-
-    def begin(i):
-        if i < len(items):
-            for copy in copies(i):
-                copy.start()
-
-    for i in range(slots):
-        begin(i)
+
+    def down_copy(n):
+        at = pl.ds(n * TILE, TILE)
+        return pltpu.make_async_copy(w_down.at[:, at], ring.at[n % slots], sems.at[n % slots])
+
+    for n in range(min(slots, blocks)):
+        down_copy(n).start()
 
     flat[...] = parts[...].astype(jnp.float32).reshape(flat.shape)
     for j in range(heads):
@@ -215,35 +171,23 @@
             pl.ds(j, tokens, stride=heads), :
         ].astype(jnp.bfloat16)
 
-    for n in range(tiles):
-        if n < first:
-            weight = held[n][...]
-        else:
-            copies(n - first)[0].wait()
-            weight = pool[(n - first) % slots]
-        product = jnp.dot(normed[...], weight, preferred_element_type=jnp.float32)
-        if n >= first:
-            begin(n - first + slots)
-        if n % 2 == 0:
-            gate = product
-        else:
-            at = slice(n // 2 * TILE, (n // 2 + 1) * TILE)
-            hidden[:, at] = (gate / (1.0 + jnp.exp(-gate)) * product).astype(jnp.bfloat16)
-
-    step = HALF_TILE
-    for i in range(tiles - first, len(items)):
-        for k, copy in enumerate(copies(i)):
-            copy.wait()
-            weight = pool[i % slots, k * local_hidden : (k + 1) * local_hidden, :]
-            part = jnp.dot(hidden[...], weight, preferred_element_type=jnp.float32)
-            block = items[i][1] + k
-            for q in range(TILE // step):
-                target, column = divmod(block * TILE + q * step, columns)
-                for g in range(tokens // group_rows):
-                    out[g * targets + target, :, column : column + step] = part[
-                        g * group_rows : (g + 1) * group_rows, q * step : (q + 1) * step
-                    ].astype(out.dtype)
-        begin(i + slots)
+    for n in range(local_hidden // TILE):
+        at = slice(n * TILE, (n + 1) * TILE)
+        gate = jnp.dot(normed[...], w_gate[:, at], preferred_element_type=jnp.float32)
+        up = jnp.dot(normed[...], w_up[:, at], preferred_element_type=jnp.float32)
+        hidden[:, at] = (gate / (1.0 + jnp.exp(-gate)) * up).astype(jnp.bfloat16)
+
+    for n in range(blocks):
+        down_copy(n).wait()
+        part = jnp.dot(hidden[...], ring[n % slots], preferred_element_type=jnp.float32)
+        if n + slots < blocks:
+            down_copy(n + slots).start()
+        for q in range(0, TILE, PART):
+            target, column = divmod(n * TILE + q, columns)
+            for g in range(tokens // group_rows):
+                out[g * targets + target, :, column : column + PART] = part[
+                    g * group_rows : (g + 1) * group_rows, q : q + PART
+                ].astype(out.dtype)
 
 
 def experts(parts, w_gate, w_up, w_down, group_rows, dev_count):
@@ -253,18 +197,18 @@
     return pl.pallas_call(
         experts_kernel,
         out_shape=jax.ShapeDtypeStruct((SHARING_DEVICES * tokens, group_rows, columns), jnp.bfloat16),
-        in_specs=[VMEM, HBM, HBM, HBM],
+        in_specs=[VMEM, VMEM, VMEM, HBM],
         out_specs=VMEM,
         scratch_shapes=[
             pltpu.VMEM((tokens * width // HEAD_SIZE, HEAD_SIZE), jnp.float32),
             pltpu.VMEM((tokens, width), jnp.bfloat16),
             pltpu.VMEM((tokens, local_hidden), jnp.bfloat16),
-            pltpu.VMEM((POOL, width, TILE), jnp.bfloat16),
-            pltpu.SemaphoreType.DMA((POOL, width // local_hidden)),
+            pltpu.VMEM((RING, local_hidden, TILE), jnp.bfloat16),
+            pltpu.SemaphoreType.DMA((RING,)),
         ],
-        compiler_params=pltpu.CompilerParams(vmem_limit_bytes=(6 * POOL + 2) * MIB),
+        compiler_params=pltpu.CompilerParams(vmem_limit_bytes=(2 * RING + 1) * MIB),
         name="experts",
-    )(*in_vmem(parts), *in_hbm(w_gate, w_up, w_down))
+    )(*in_vmem(parts, w_gate, w_up), *in_hbm(w_down))
 
 
 def experts_plain(parts, w_gate, w_up, w_down, group_rows, dev_count):
@@ -325,18 +269,15 @@
     chips = lax.axis_size("grp") * lax.axis_size("pair")
     dev_count = lax.axis_size("pair") * SHARING_DEVICES
     group_rows = residual.shape[0]
-    streamed = w_gate.shape[1] == 4 * TILE
-    summed, *early = attend(
-        lengths, queries, cached_key_rows, cached_value_rows, incoming_keys, incoming_values,
-        residual, w_gate, w_up, EARLY_TILES if streamed else 0,
+    summed = attend(
+        lengths, queries, cached_key_rows, cached_value_rows, incoming_keys, incoming_values, residual
     )
     other = lax.ppermute(summed, "half", [(0, 1), (1, 0)])
     sent = norm(summed, other, norm_gain, chips)
     rows = lax.all_to_all(sent, ("grp", "pair"), 0, 0, tiled=True)
-    if streamed:
-        part = experts(rows, *early, w_gate, w_up, w_down, group_rows, dev_count)
-    else:
-        part = experts_plain(rows, w_gate, w_up, w_down, group_rows, dev_count)
+    whole_blocks = w_gate.shape[1] % TILE == 0 and norm_gain.shape[0] // dev_count % PART == 0
+    run_experts = experts if whole_blocks else experts_plain
+    part = run_experts(rows, w_gate, w_up, w_down, group_rows, dev_count)
     got = lax.all_to_all(part, ("grp", "pair", "half"), 0, 0, tiled=True)
     return combine(got, expert_ids, route_logits, dev_count)
 

time: 58.7 us -> 47.6 us (0.81)
  Pallas kernels: 27.1 us -> 16.5 us
  local copies, waits for them, and re-layouts: 0.93 us -> 0.2 us
    pallas_call x1, Pallas kernels: 24.4 us -> 13.6 us  [experts(): pl.pallas_call(experts_kernel, out_shape=jax.ShapeDtypeStruct((SHARING_DE...]
    unnamed x8 -> x12, local copies, waits for them, and re-layouts: 0.93 us -> 0.2 us
where the time goes in v3:
time: 47.6 us; the launch traced here: 47.4 us
  Pallas kernels  16.5 us (35%)
  blocking collectives  14.8 us (31%)
  waiting for transfers between devices  10.4 us (22%)
  starting transfers between devices  5.46 us (11%)
    all_to_all x1, blocking collectives, body(): rows = lax.all_to_all(sent, ('grp', 'pair'), 0, 0, tiled=True)  14.8 us
    pallas_call x1, Pallas kernels, experts(): pl.pallas_call(experts_kernel, out_shape=jax.ShapeDtypeStruct((SHARING_DE...  13.6 us
    all_to_all x1, waiting for transfers between devices, body(): got = lax.all_to_all(part, ('grp', 'pair', 'half'), 0, 0, tiled=True)  9.23 us
    all_to_all x1, starting transfers between devices, body(): got = lax.all_to_all(part, ('grp', 'pair', 'half'), 0, 0, tiled=True)  5.35 us
    pallas_call x1, Pallas kernels, attend(): pl.pallas_call(attend_kernel, out_shape=jax.ShapeDtypeStruct((LOCAL_HEADS...  1.91 us
    ppermute x1, waiting for transfers between devices, body(): other = lax.ppermute(summed, 'half', [(0, 1), (1, 0)])  1.13 us
  transfers between devices with their start and end apart: 2, of which 2 were waited for; matrix products, arithmetic and copies ran while one was open for 0% of the time, Pallas kernels for 0%

profile of v3, /device:TPU:1, one launch (start us, length us, event | category | flops | bytes accessed | tf_op | source)
XLA Modules:
  0.0 47.4 jit_solution(4231161206714687000)
XLA Ops:
  0.0 0.0 copy-start.2
  0.0 0.0 copy-start
  0.0 0.0 copy-start.1
  0.0 1.9 %attend.1.mine = f32[24,128]{1,0:T(8,128)S(1)} custom-call(s32[4]{0:T(128)} %lengths.1, bf16[1,3072]{1,0:T(2,128)(2,1)} %queries.1, bf16[1,512,512]{2,1,0:T(8,128)(2,1)} %key_rows.1, bf16[1,512,512]{2,1,0:T(8,128)(2,1)} %value_rows.1, bf16[1,512]{1,0:T(2,128)(2,1)} %new_keys.1, bf16[1,512]{1,0:T(2,128)(2,1)} %new_values.1, bf16[4,6144]{1,0:T(4,128)(2,1)} %residual.1), custom_call_target="tpu_custom_call" | custom-call | flops 40000000000 | tf_op jit(solution)/shard_map/attend/pallas_call | solution.py:109
  1.9 0.1 collective-permute-start
  2.0 1.1 %collective-permute-done.other = f32[24,128]{1,0:T(8,128)S(1)} collective-permute-done((f32[24,128]{1,0:T(8,128)S(1)}, f32[24,128]{1,0:T(8,128)S(1)}, u32[]{:S(2)}, u32[]{:S(2)}) %collective-permute-start) | collective-permute-done | bytes 12320 | tf_op jit(solution)/shard_map/ppermute | solution.py:275
  3.2 0.0 copy-done.2
  3.2 0.1 norm.1
  3.3 14.8 %all_to_all.10.parts = bf16[16,48,128]{2,1,0:T(8,128)(2,1)S(1)} all-to-all(bf16[16,48,128]{2,1,0:T(8,128)(2,1)S(1)} %norm.1), channel_id=1, replica_groups=mesh['grp'=4,'pair'=4,'half'=2] {'grp','pair'}, dimensions={0} | all-to-all | bytes 393216 | tf_op jit(solution)/shard_map/all_to_all | solution.py:277
  18.1 0.0 copy-done
  18.1 0.0 copy-done.1
  18.1 0.0 copy-start.3
  18.1 0.0 copy-start.4
  18.1 13.6 %experts.1 = bf16[32,4,768]{2,1,0:T(4,128)(2,1)} custom-call(bf16[16,48,128]{2,1,0:T(8,128)(2,1)S(1)} %all_to_all.10.parts, bf16[6144,2048]{1,0:T(8,128)(2,1)S(1)} %copy-done, bf16[6144,2048]{1,0:T(8,128)(2,1)S(1)} %copy-done.1, bf16[2048,6144]{1,0:T(8,128)(2,1)} %w_down.1), custom_call_target="tpu_custom_call" | custom-call | tf_op jit(solution)/shard_map/experts/pallas_call | solution.py:197
  31.7 5.3 %all-to-all-start.1 = ((bf16[32,4,768]{2,1,0:T(4,128)(2,1)}), bf16[32,4,768]{2,1,0:T(4,128)(2,1)S(1)}, u32[]{:S(2)}, u32[]{:S(2)}) async-start(bf16[32,4,768]{2,1,0:T(4,128)(2,1)} %experts.1), calls=%async_computation.1 | async-start | bytes 393216 | tf_op jit(solution)/shard_map/all_to_all | solution.py:281
  37.1 0.0 copy-done.3
  37.1 0.1 copy.14.ids
  37.2 0.0 copy-done.4
  37.2 0.1 copy.15.logits
  37.3 9.2 %all-to-all-done.1.parts = bf16[32,4,768]{2,1,0:T(4,128)(2,1)S(1)} async-done(((bf16[32,4,768]{2,1,0:T(4,128)(2,1)}), bf16[32,4,768]{2,1,0:T(4,128)(2,1)S(1)}, u32[]{:S(2)}, u32[]{:S(2)}) %all-to-all-start.1) | async-done | bytes 196640 | tf_op jit(solution)/shard_map/all_to_all | solution.py:281
  46.5 0.9 %combine.1 = bf16[4,768]{1,0:T(4,128)(2,1)} custom-call(bf16[32,4,768]{2,1,0:T(4,128)(2,1)S(1)} %all-to-all-done.1.parts, s32[4,2]{1,0:T(4,128)S(1)} %copy.14.ids, f32[4,2]{1,0:T(4,128)S(1)} %copy.15.logits), custom_call_target="tpu_custom_call" | custom-call | tf_op jit(solution)/shard_map/combine/pallas_call | solution.py:244
Async XLA Ops:
  0.0 3.2 %copy-start.2 = (f32[6144]{0:T(1024)S(1)}, f32[6144]{0:T(1024)}, u32[]{:S(2)}) copy-start(f32[6144]{0:T(1024)} %param.20) | copy-start | bytes 73732
  0.0 18.1 %copy-start = (bf16[6144,2048]{1,0:T(8,128)(2,1)S(1)}, bf16[6144,2048]{1,0:T(8,128)(2,1)}, u32[]{:S(2)}) copy-start(bf16[6144,2048]{1,0:T(8,128)(2,1)} %w_gate.1) | copy-start | bytes 75497472
  0.0 18.1 %copy-start.1 = (bf16[6144,2048]{1,0:T(8,128)(2,1)S(1)}, bf16[6144,2048]{1,0:T(8,128)(2,1)}, u32[]{:S(2)}) copy-start(bf16[6144,2048]{1,0:T(8,128)(2,1)} %w_up.1) | copy-start | bytes 75497472
  1.9 1.2 %collective-permute-start = (f32[24,128]{1,0:T(8,128)S(1)}, f32[24,128]{1,0:T(8,128)S(1)}, u32[]{:S(2)}, u32[]{:S(2)}) collective-permute-start(f32[24,128]{1,0:T(8,128)S(1)} %attend.1.mine), channel_id=1, source_target_pairs={{0,1},{1,0},{2,3},{3,2},{4,5},{5,4},{6,7},{7,6},{8,9},{9,8},{10,11... | collective-permute-start | bytes 36872 | tf_op jit(solution)/shard_map/ppermute | solution.py:275
  18.1 19.0 %copy-start.3 = (s32[4,2]{0,1:T(2,128)S(1)}, s32[4,2]{0,1:T(2,128)}, u32[]{:S(2)}) copy-start(s32[4,2]{0,1:T(2,128)} %param.21) | copy-start | bytes 100
  18.1 19.1 %copy-start.4 = (f32[4,2]{0,1:T(2,128)S(1)}, f32[4,2]{0,1:T(2,128)}, u32[]{:S(2)}) copy-start(f32[4,2]{0,1:T(2,128)} %param.22) | copy-start | bytes 100
  31.7 14.8 %all-to-all-start.1 = ((bf16[32,4,768]{2,1,0:T(4,128)(2,1)}), bf16[32,4,768]{2,1,0:T(4,128)(2,1)S(1)}, u32[]{:S(2)}, u32[]{:S(2)}) async-start(bf16[32,4,768]{2,1,0:T(4,128)(2,1)} %experts.1), calls=%async_computation.1 | async-start | bytes 393216 | tf_op jit(solution)/shard_map/all_to_all | solution.py:281

commit v4 on v3

--- a/solution.py
+++ b/solution.py
@@ -20,6 +20,8 @@
 TILE = 512
 PART = 256
 RING = 6
+PASSES = 2
+DOWN = 1024
 UNTIL_ROWS = pl.CostEstimate(flops=40_000_000_000, bytes_accessed=0, transcendentals=0)
 
 
@@ -38,9 +40,14 @@
     )
 
 
+def as_column(row, diagonal):
+    return jnp.sum(jnp.where(diagonal, row, jnp.zeros_like(row)), axis=1, keepdims=True)
+
+
 def attend_kernel(
-    lengths, queries, key_rows, value_rows, new_keys, new_values, residual, out,
-    length_buf, query_buf, key_buf, value_buf, new_key_buf, new_value_buf, residual_buf, sems,
+    lengths, queries, key_rows, value_rows, new_keys, new_values, residual, ids, logits, out, weights_out,
+    length_buf, query_buf, key_buf, value_buf, new_key_buf, new_value_buf, residual_buf, id_buf, logit_buf,
+    sems,
 ):
     sequence, half = lax.axis_index("pair"), lax.axis_index("half")
     heads = LOCAL_HEADS
@@ -54,6 +61,8 @@
         (new_values, new_value_buf),
         (value_rows.at[0], value_buf),
         (residual.at[:, at], residual_buf),
+        (ids, id_buf),
+        (logits, logit_buf),
     ]
     copies = [pltpu.make_async_copy(*pair, sems.at[i]) for i, pair in enumerate(pairs)]
     for copy in copies:
@@ -102,15 +111,33 @@
     mine = jnp.sum(jnp.where(rows == sequence, mine, 0.0), axis=0, keepdims=True)
     out[...] = attended + head_rows(mine)
 
-
-def attend(lengths, queries, key_rows, value_rows, new_keys, new_values, residual):
+    count, tokens = id_buf.shape
+    diagonal = lax.broadcasted_iota(jnp.int32, (tokens, tokens), 0) == lax.broadcasted_iota(
+        jnp.int32, (tokens, tokens), 1
+    )
+    chosen = [as_column(id_buf[k : k + 1, :], diagonal) for k in range(count)]
+    logit = [as_column(logit_buf[k : k + 1, :], diagonal) for k in range(count)]
+    top = functools.reduce(jnp.maximum, logit)
+    raised = [jnp.exp(v - top) for v in logit]
+    scale = 1.0 / functools.reduce(jnp.add, raised)
+    expert = lax.broadcasted_iota(jnp.int32, weights_out.shape, 1)
+    by_expert = jnp.zeros(weights_out.shape, jnp.float32)
+    for k in range(count):
+        by_expert = by_expert + jnp.where(chosen[k] == expert, raised[k] * scale, 0.0)
+    weights_out[...] = by_expert
+
+
+def attend(lengths, queries, key_rows, value_rows, new_keys, new_values, residual, ids, logits):
     half_columns = LOCAL_HEADS * HEAD_SIZE
-    operands = [lengths, queries, key_rows, value_rows, new_keys, new_values, residual]
+    operands = [lengths, queries, key_rows, value_rows, new_keys, new_values, residual, ids.T, logits.T]
     return pl.pallas_call(
         attend_kernel,
-        out_shape=jax.ShapeDtypeStruct((LOCAL_HEADS, HEAD_SIZE), jnp.float32),
+        out_shape=(
+            jax.ShapeDtypeStruct((LOCAL_HEADS, HEAD_SIZE), jnp.float32),
+            jax.ShapeDtypeStruct((ids.shape[0], E), jnp.float32),
+        ),
         in_specs=[HBM] * len(operands),
-        out_specs=VMEM,
+        out_specs=(VMEM, VMEM),
         scratch_shapes=[
             pltpu.SMEM(lengths.shape, jnp.int32),
             pltpu.VMEM(queries.shape, jnp.bfloat16),
@@ -119,7 +146,9 @@
             pltpu.VMEM(new_keys.shape, jnp.bfloat16),
             pltpu.VMEM(new_values.shape, jnp.bfloat16),
             pltpu.VMEM((residual.shape[0], half_columns), jnp.bfloat16),
-            pltpu.SemaphoreType.DMA((7,)),
+            pltpu.VMEM(ids.shape[::-1], jnp.int32),
+            pltpu.VMEM(logits.shape[::-1], jnp.float32),
+            pltpu.SemaphoreType.DMA((len(operands),)),
         ],
         compiler_params=pltpu.CompilerParams(vmem_limit_bytes=4 * MIB),
         cost_estimate=UNTIL_ROWS,
@@ -150,20 +179,24 @@
     )(mine, other, gain.reshape(heads, HEAD_SIZE))
 
 
-def experts_kernel(parts, w_gate, w_up, w_down, out, flat, normed, hidden, ring, sems):
+def experts_kernel(
+    parts, w_gate, w_up, w_down, out, flat, normed, hidden, total, ring, sems
+):
     tokens, width = normed.shape
-    local_hidden = w_down.shape[0]
-    slots, heads = ring.shape[0], width // HEAD_SIZE
+    local_hidden = hidden.shape[1]
+    slots, units = ring.shape[:2]
+    heads = width // HEAD_SIZE
     group_rows, columns = out.shape[1:]
     targets = width // columns
-    blocks = width // TILE
-
-    def down_copy(n):
-        at = pl.ds(n * TILE, TILE)
-        return pltpu.make_async_copy(w_down.at[:, at], ring.at[n % slots], sems.at[n % slots])
-
-    for n in range(min(slots, blocks)):
-        down_copy(n).start()
+    blocks = width // DOWN
+
+    def down_copy(i):
+        which, n = divmod(i, blocks)
+        source = w_down.at[pl.ds(which * units, units), pl.ds(n * DOWN, DOWN)]
+        return pltpu.make_async_copy(source, ring.at[i % slots], sems.at[i % slots])
+
+    for i in range(min(slots, PASSES * blocks)):
+        down_copy(i).start()
 
     flat[...] = parts[...].astype(jnp.float32).reshape(flat.shape)
     for j in range(heads):
@@ -171,29 +204,38 @@
             pl.ds(j, tokens, stride=heads), :
         ].astype(jnp.bfloat16)
 
-    for n in range(local_hidden // TILE):
-        at = slice(n * TILE, (n + 1) * TILE)
-        gate = jnp.dot(normed[...], w_gate[:, at], preferred_element_type=jnp.float32)
-        up = jnp.dot(normed[...], w_up[:, at], preferred_element_type=jnp.float32)
-        hidden[:, at] = (gate / (1.0 + jnp.exp(-gate)) * up).astype(jnp.bfloat16)
-
-    for n in range(blocks):
-        down_copy(n).wait()
-        part = jnp.dot(hidden[...], ring[n % slots], preferred_element_type=jnp.float32)
-        if n + slots < blocks:
-            down_copy(n + slots).start()
-        for q in range(0, TILE, PART):
-            target, column = divmod(n * TILE + q, columns)
-            for g in range(tokens // group_rows):
-                out[g * targets + target, :, column : column + PART] = part[
-                    g * group_rows : (g + 1) * group_rows, q : q + PART
-                ].astype(out.dtype)
+    for which in range(PASSES):
+        mine = slice(which * units, (which + 1) * units)
+        for start in range(which * units, (which + 1) * units, TILE):
+            at = slice(start, start + TILE)
+            gate = jnp.dot(normed[...], w_gate[:, at], preferred_element_type=jnp.float32)
+            up = jnp.dot(normed[...], w_up[:, at], preferred_element_type=jnp.float32)
+            hidden[:, at] = (gate / (1.0 + jnp.exp(-gate)) * up).astype(jnp.bfloat16)
+        for n in range(blocks):
+            i = which * blocks + n
+            down_copy(i).wait()
+            part = jnp.dot(hidden[:, mine], ring[i % slots], preferred_element_type=jnp.float32)
+            if i + slots < PASSES * blocks:
+                down_copy(i + slots).start()
+            at = slice(n * DOWN, (n + 1) * DOWN)
+            if which > 0:
+                part = total[:, at] + part
+            if which < PASSES - 1:
+                total[:, at] = part
+                continue
+            for q in range(0, DOWN, PART):
+                target, column = divmod(n * DOWN + q, columns)
+                for g in range(tokens // group_rows):
+                    out[g * targets + target, :, column : column + PART] = part[
+                        g * group_rows : (g + 1) * group_rows, q : q + PART
+                    ].astype(out.dtype)
 
 
 def experts(parts, w_gate, w_up, w_down, group_rows, dev_count):
     tokens = parts.shape[0]
     width, local_hidden = w_gate.shape
     columns = width // dev_count
+    units = local_hidden // PASSES
     return pl.pallas_call(
         experts_kernel,
         out_shape=jax.ShapeDtypeStruct((SHARING_DEVICES * tokens, group_rows, columns), jnp.bfloat16),
@@ -203,10 +245,11 @@
             pltpu.VMEM((tokens * width // HEAD_SIZE, HEAD_SIZE), jnp.float32),
             pltpu.VMEM((tokens, width), jnp.bfloat16),
             pltpu.VMEM((tokens, local_hidden), jnp.bfloat16),
-            pltpu.VMEM((RING, local_hidden, TILE), jnp.bfloat16),
+            pltpu.VMEM((tokens, width), jnp.float32),
+            pltpu.VMEM((RING, units, DOWN), jnp.bfloat16),
             pltpu.SemaphoreType.DMA((RING,)),
         ],
-        compiler_params=pltpu.CompilerParams(vmem_limit_bytes=(2 * RING + 1) * MIB),
+        compiler_params=pltpu.CompilerParams(vmem_limit_bytes=RING * units * DOWN * 2 + 2 * MIB),
         name="experts",
     )(*in_vmem(parts, w_gate, w_up), *in_hbm(w_down))
 
@@ -222,33 +265,28 @@
     return part.transpose(0, 2, 1, 3).reshape(-1, group_rows, width // dev_count)
 
 
-def combine_kernel(per_expert, dev_count, parts, ids, logits, out):
+def combine_kernel(per_expert, dev_count, parts, weights, out):
     shards = parts.shape[0] // dev_count
-    logit = logits[...]
-    top = jnp.max(logit, axis=1, keepdims=True)
-    raised = jnp.exp(logit - top)
-    probs = raised / jnp.sum(raised, axis=1, keepdims=True)
-    chosen = ids[...]
+    weight = weights[...]
     total = jnp.zeros(out.shape, jnp.float32)
     for e in range(E):
-        weight = jnp.sum(jnp.where(chosen == e, probs, 0.0), axis=1, keepdims=True)
         here = jnp.zeros(out.shape, jnp.float32)
         for g in range(shards):
             for c in range(per_expert):
                 here = here + parts[g * dev_count + e * per_expert + c].astype(jnp.float32)
-        total = total + weight * here
+        total = total + weight[:, e : e + 1] * here
     out[...] = total.astype(out.dtype)
 
 
-def combine(parts, ids, logits, dev_count):
+def combine(parts, weights, dev_count):
     return pl.pallas_call(
         functools.partial(combine_kernel, dev_count // E, dev_count),
         out_shape=jax.ShapeDtypeStruct(parts.shape[1:], jnp.bfloat16),
-        in_specs=[VMEM] * 3,
+        in_specs=[VMEM] * 2,
         out_specs=VMEM,
         compiler_params=pltpu.CompilerParams(vmem_limit_bytes=24 * MIB),
         name="combine",
-    )(parts, ids, logits)
+    )(*in_vmem(parts, weights))
 
 
 def body(
@@ -269,17 +307,18 @@
     chips = lax.axis_size("grp") * lax.axis_size("pair")
     dev_count = lax.axis_size("pair") * SHARING_DEVICES
     group_rows = residual.shape[0]
-    summed = attend(
-        lengths, queries, cached_key_rows, cached_value_rows, incoming_keys, incoming_values, residual
+    summed, weights = attend(
+        lengths, queries, cached_key_rows, cached_value_rows, incoming_keys, incoming_values,
+        residual, expert_ids, route_logits,
     )
     other = lax.ppermute(summed, "half", [(0, 1), (1, 0)])
     sent = norm(summed, other, norm_gain, chips)
     rows = lax.all_to_all(sent, ("grp", "pair"), 0, 0, tiled=True)
-    whole_blocks = w_gate.shape[1] % TILE == 0 and norm_gain.shape[0] // dev_count % PART == 0
+    whole_blocks = w_gate.shape[1] % (PASSES * TILE) == 0 and norm_gain.shape[0] // dev_count % PART == 0
     run_experts = experts if whole_blocks else experts_plain
     part = run_experts(rows, w_gate, w_up, w_down, group_rows, dev_count)
     got = lax.all_to_all(part, ("grp", "pair", "half"), 0, 0, tiled=True)
-    return combine(got, expert_ids, route_logits, dev_count)
+    return combine(got, weights, dev_count)
 
 
 def solution(mesh):

time: 47.6 us -> 45.4 us (0.954)
  blocking collectives: 14.8 us -> 29.6 us
  waiting for transfers between devices: 10.4 us -> 1.13 us
  starting transfers between devices: 5.46 us -> 0.12 us
  Pallas kernels: 16.5 us -> 14.4 us
    all_to_all x0 -> x1, blocking collectives: none -> 14.8 us  [body(): got = lax.all_to_all(part, ('grp', 'pair', 'half'), 0, 0, tiled=True)]
    all_to_all x1 -> x0, waiting for transfers between devices: 9.23 us -> none  [body(): got = lax.all_to_all(part, ('grp', 'pair', 'half'), 0, 0, tiled=True)]
    all_to_all x1 -> x0, starting transfers between devices: 5.35 us -> none  [body(): got = lax.all_to_all(part, ('grp', 'pair', 'half'), 0, 0, tiled=True)]
    pallas_call x1, Pallas kernels: 13.6 us -> 11.7 us  [experts(): pl.pallas_call(experts_kernel, out_shape=jax.ShapeDtypeStruct((SHARING_DE...]
  transfers between devices with their start and end apart: 2 -> 1, of which waited for: 2 -> 1; matrix products, arithmetic and copies ran while one was open for 0% -> 0% of each run, Pallas kernels for 0% -> 0%
where the time goes in v4:
time: 45.4 us; the launch traced here: 45.2 us
  blocking collectives  29.6 us (65%)
  Pallas kernels  14.4 us (32%)
  waiting for transfers between devices  1.13 us (2%)
    all_to_all x1, blocking collectives, body(): rows = lax.all_to_all(sent, ('grp', 'pair'), 0, 0, tiled=True)  14.8 us
    all_to_all x1, blocking collectives, body(): got = lax.all_to_all(part, ('grp', 'pair', 'half'), 0, 0, tiled=True)  14.8 us
    pallas_call x1, Pallas kernels, experts(): pl.pallas_call(experts_kernel, out_shape=jax.ShapeDtypeStruct((SHARING_DE...  11.7 us
    pallas_call x1, Pallas kernels, attend(): pl.pallas_call(attend_kernel, out_shape=(jax.ShapeDtypeStruct((LOCAL_HEAD...  1.93 us
    ppermute x1, waiting for transfers between devices, body(): other = lax.ppermute(summed, 'half', [(0, 1), (1, 0)])  1.13 us
  transfers between devices with their start and end apart: 1, of which 1 were waited for; matrix products, arithmetic and copies ran while one was open for 0% of the time, Pallas kernels for 0%

profile of v4, /device:TPU:1, one launch (start us, length us, event | category | flops | bytes accessed | tf_op | source)
XLA Modules:
  0.0 45.2 jit_solution(2853056671011128183)
XLA Ops:
  0.0 0.0 copy-start.2
  0.0 0.0 copy-start
  0.0 0.0 copy-start.1
  0.0 1.9 %attend.1 = (f32[24,128]{1,0:T(8,128)S(1)}, f32[4,8]{1,0:T(4,128)S(1)}) custom-call(s32[4]{0:T(128)} %lengths.1, bf16[1,3072]{1,0:T(2,128)(2,1)} %queries.1, bf16[1,512,512]{2,1,0:T(8,128)(2,1)} %key_rows.1, bf16[1,512,512]{2,1,0:T(8,128)(2,1)} %value_rows.1, bf16[1,512]{1,0:T(2,128)(2,1)} %new_keys.1, bf16[1,512]{1,0:T(2,128)(2,1)} %new_values.1, ...), custom_call_target="tpu_custom_call" | custom-call | flops 40000000000 | tf_op jit(solution)/shard_map/attend/pallas_call | solution.py:133
  2.0 0.1 collective-permute-start
  2.1 1.1 %collective-permute-done.other = f32[24,128]{1,0:T(8,128)S(1)} collective-permute-done((f32[24,128]{1,0:T(8,128)S(1)}, f32[24,128]{1,0:T(8,128)S(1)}, u32[]{:S(2)}, u32[]{:S(2)}) %collective-permute-start) | collective-permute-done | bytes 12320 | tf_op jit(solution)/shard_map/ppermute | solution.py:314
  3.2 0.0 copy-done.2
  3.2 0.1 norm.1
  3.3 14.8 %all_to_all.10.parts = bf16[16,48,128]{2,1,0:T(8,128)(2,1)S(1)} all-to-all(bf16[16,48,128]{2,1,0:T(8,128)(2,1)S(1)} %norm.1), channel_id=1, replica_groups=mesh['grp'=4,'pair'=4,'half'=2] {'grp','pair'}, dimensions={0} | all-to-all | bytes 393216 | tf_op jit(solution)/shard_map/all_to_all | solution.py:316
  18.1 0.0 copy-done
  18.1 0.0 copy-done.1
  18.1 11.7 %experts.1 = bf16[32,4,768]{2,1,0:T(4,128)(2,1)} custom-call(bf16[16,48,128]{2,1,0:T(8,128)(2,1)S(1)} %all_to_all.10.parts, bf16[6144,2048]{1,0:T(8,128)(2,1)S(1)} %copy-done, bf16[6144,2048]{1,0:T(8,128)(2,1)S(1)} %copy-done.1, bf16[2048,6144]{1,0:T(8,128)(2,1)} %w_down.1), custom_call_target="tpu_custom_call" | custom-call | tf_op jit(solution)/shard_map/experts/pallas_call | solution.py:239
  29.8 14.8 %all_to_all.11.parts = bf16[32,4,768]{2,1,0:T(4,128)(2,1)S(1)} all-to-all(bf16[32,4,768]{2,1,0:T(4,128)(2,1)} %experts.1), channel_id=1, replica_groups=mesh['grp'=4,'pair'=4,'half'=2] {'grp','pair','half'}, dimensions={0} | all-to-all | bytes 393216 | tf_op jit(solution)/shard_map/all_to_all | solution.py:320
  44.5 0.7 %combine.1 = bf16[4,768]{1,0:T(4,128)(2,1)} custom-call(bf16[32,4,768]{2,1,0:T(4,128)(2,1)S(1)} %all_to_all.11.parts, f32[4,8]{1,0:T(4,128)S(1)} %get-tuple-element.8.weights), custom_call_target="tpu_custom_call" | custom-call | tf_op jit(solution)/shard_map/combine/pallas_call | solution.py:282
Async XLA Ops:
  0.0 3.2 %copy-start.2 = (f32[6144]{0:T(1024)S(1)}, f32[6144]{0:T(1024)}, u32[]{:S(2)}) copy-start(f32[6144]{0:T(1024)} %param.20) | copy-start | bytes 73732
  0.0 18.1 %copy-start = (bf16[6144,2048]{1,0:T(8,128)(2,1)S(1)}, bf16[6144,2048]{1,0:T(8,128)(2,1)}, u32[]{:S(2)}) copy-start(bf16[6144,2048]{1,0:T(8,128)(2,1)} %w_gate.1) | copy-start | bytes 75497472
  0.0 18.1 %copy-start.1 = (bf16[6144,2048]{1,0:T(8,128)(2,1)S(1)}, bf16[6144,2048]{1,0:T(8,128)(2,1)}, u32[]{:S(2)}) copy-start(bf16[6144,2048]{1,0:T(8,128)(2,1)} %w_up.1) | copy-start | bytes 75497472
  2.0 1.2 %collective-permute-start = (f32[24,128]{1,0:T(8,128)S(1)}, f32[24,128]{1,0:T(8,128)S(1)}, u32[]{:S(2)}, u32[]{:S(2)}) collective-permute-start(f32[24,128]{1,0:T(8,128)S(1)} %get-tuple-element.7.mine), channel_id=1, source_target_pairs={{0,1},{1,0},{2,3},{3,2},{4,5},{5,4},{6,7},{7,6},{8,9},{9,8},{10,11... | collective-permute-start | bytes 36872 | tf_op jit(solution)/shard_map/ppermute | solution.py:314

commit v5 on v4

--- a/solution.py
+++ b/solution.py
@@ -17,6 +17,7 @@
 MIB = 2**20
 VMEM = pl.BlockSpec(memory_space=pltpu.VMEM)
 HBM = pl.BlockSpec(memory_space=pltpu.HBM)
+MXU = 256
 TILE = 512
 PART = 256
 RING = 6
@@ -179,11 +180,50 @@
     )(mine, other, gain.reshape(heads, HEAD_SIZE))
 
 
+class Job:
+    def __init__(self, rows, weight, before, after, after_rows):
+        self.rows, self.weight, self.before, self.after = rows, weight, before, after
+        self.after_rows = after_rows
+
+
+def run_jobs(jobs, sums):
+    steps = [(n, k) for n, job in enumerate(jobs) for k in range(0, job.rows.shape[1], MXU)]
+
+    def push(i):
+        n, k = steps[i]
+        job = jobs[n]
+        if k == 0:
+            job.before()
+        for m in range(2):
+            tile = job.weight[k : k + MXU, m * MXU : (m + 1) * MXU]
+            pltpu.matmul_push_rhs(tile, i % 2, m)
+
+    pending = []
+
+    def settle():
+        while pending:
+            n = pending.pop()
+            jobs[n].after([pltpu.matmul_pop(sums[n % 2][m]) for m in range(2)])
+
+    push(0)
+    for i, (n, k) in enumerate(steps):
+        if i + 1 < len(steps):
+            push(i + 1)
+        job = jobs[n]
+        if k == 0 and job.after_rows:
+            settle()
+        for m in range(2):
+            pltpu.matmul_acc_lhs(sums[n % 2][m], job.rows[:, k : k + MXU], load_staged_rhs=i % 2)
+        settle()
+        if k + MXU == job.rows.shape[1]:
+            pending.append(n)
+    settle()
+
+
 def experts_kernel(
-    parts, w_gate, w_up, w_down, out, flat, normed, hidden, total, ring, sems
+    parts, w_gate, w_up, w_down, out, flat, normed, hidden, gates, total, ring, sems
 ):
     tokens, width = normed.shape
-    local_hidden = hidden.shape[1]
     slots, units = ring.shape[:2]
     heads = width // HEAD_SIZE
     group_rows, columns = out.shape[1:]
@@ -204,31 +244,70 @@
             pl.ds(j, tokens, stride=heads), :
         ].astype(jnp.bfloat16)
 
+    def nothing():
+        pass
+
+    def gate_done(start):
+        def after(sums):
+            for m in range(2):
+                gates[:, m * MXU : (m + 1) * MXU] = sums[m]
+
+        return after
+
+    def up_done(start):
+        def after(sums):
+            for m in range(2):
+                gate = gates[:, m * MXU : (m + 1) * MXU]
+                at = slice(start + m * MXU, start + (m + 1) * MXU)
+                hidden[:, at] = (gate / (1.0 + jnp.exp(-gate)) * sums[m]).astype(jnp.bfloat16)
+
+        return after
+
+    def down_done(which, i, start):
+        def after(sums):
+            for m in range(2):
+                column = start + m * MXU
+                part = sums[m]
+                at = slice(column, column + MXU)
+                if which > 0:
+                    part = total[:, at] + part
+                if which < PASSES - 1:
+                    total[:, at] = part
+                    continue
+                target, place = divmod(column, columns)
+                for g in range(tokens // group_rows):
+                    out[g * targets + target, :, place : place + MXU] = part[
+                        g * group_rows : (g + 1) * group_rows
+                    ].astype(out.dtype)
+            if (start + 2 * MXU) % DOWN == 0 and i + slots < PASSES * blocks:
+                down_copy(i + slots).start()
+
+        return after
+
+    jobs = []
     for which in range(PASSES):
-        mine = slice(which * units, (which + 1) * units)
-        for start in range(which * units, (which + 1) * units, TILE):
-            at = slice(start, start + TILE)
-            gate = jnp.dot(normed[...], w_gate[:, at], preferred_element_type=jnp.float32)
-            up = jnp.dot(normed[...], w_up[:, at], preferred_element_type=jnp.float32)
-            hidden[:, at] = (gate / (1.0 + jnp.exp(-gate)) * up).astype(jnp.bfloat16)
+        for start in range(which * units, (which + 1) * units, 2 * MXU):
+            at = pl.ds(start, 2 * MXU)
+            jobs.append(Job(normed, w_gate.at[:, at], nothing, gate_done(start), False))
+            jobs.append(Job(normed, w_up.at[:, at], nothing, up_done(start), False))
+        mine = hidden.at[:, pl.ds(which * units, units)]
         for n in range(blocks):
             i = which * blocks + n
-            down_copy(i).wait()
-            part = jnp.dot(hidden[:, mine], ring[i % slots], preferred_element_type=jnp.float32)
-            if i + slots < PASSES * blocks:
-                down_copy(i + slots).start()
-            at = slice(n * DOWN, (n + 1) * DOWN)
-            if which > 0:
-                part = total[:, at] + part
-            if which < PASSES - 1:
-                total[:, at] = part
-                continue
-            for q in range(0, DOWN, PART):
-                target, column = divmod(n * DOWN + q, columns)
-                for g in range(tokens // group_rows):
-                    out[g * targets + target, :, column : column + PART] = part[
-                        g * group_rows : (g + 1) * group_rows, q : q + PART
-                    ].astype(out.dtype)
+            for start in range(0, DOWN, 2 * MXU):
+                jobs.append(
+                    Job(
+                        mine,
+                        ring.at[i % slots, :, pl.ds(start, 2 * MXU)],
+                        down_copy(i).wait if start == 0 else nothing,
+                        down_done(which, i, n * DOWN + start),
+                        n == 0 and start == 0,
+                    )
+                )
+
+    pl.run_scoped(
+        lambda a, b, c, d: run_jobs(jobs, [[a, b], [c, d]]),
+        *[pltpu.ACC(m)((tokens, MXU), jnp.float32) for _ in range(2) for m in range(2)],
+    )
 
 
 def experts(parts, w_gate, w_up, w_down, group_rows, dev_count):
@@ -245,6 +324,7 @@
             pltpu.VMEM((tokens * width // HEAD_SIZE, HEAD_SIZE), jnp.float32),
             pltpu.VMEM((tokens, width), jnp.bfloat16),
             pltpu.VMEM((tokens, local_hidden), jnp.bfloat16),
+            pltpu.VMEM((tokens, 2 * MXU), jnp.float32),
             pltpu.VMEM((tokens, width), jnp.float32),
             pltpu.VMEM((RING, units, DOWN), jnp.bfloat16),
             pltpu.SemaphoreType.DMA((RING,)),

time: 45.4 us -> 44.6 us (0.982)
  Pallas kernels: 14.4 us -> 13.5 us
    pallas_call x1, Pallas kernels: 11.7 us -> 10.8 us  [experts(): pl.pallas_call(experts_kernel, out_shape=jax.ShapeDtypeStruct((SHARING_DE...]
where the time goes in v5:
time: 44.6 us; the launch traced here: 44.4 us
  blocking collectives  29.6 us (66%)
  Pallas kernels  13.5 us (30%)
  waiting for transfers between devices  1.13 us (3%)
    all_to_all x1, blocking collectives, body(): rows = lax.all_to_all(sent, ('grp', 'pair'), 0, 0, tiled=True)  14.8 us
    all_to_all x1, blocking collectives, body(): got = lax.all_to_all(part, ('grp', 'pair', 'half'), 0, 0, tiled=True)  14.8 us
    pallas_call x1, Pallas kernels, experts(): pl.pallas_call(experts_kernel, out_shape=jax.ShapeDtypeStruct((SHARING_DE...  10.8 us
    pallas_call x1, Pallas kernels, attend(): pl.pallas_call(attend_kernel, out_shape=(jax.ShapeDtypeStruct((LOCAL_HEAD...  1.93 us
    ppermute x1, waiting for transfers between devices, body(): other = lax.ppermute(summed, 'half', [(0, 1), (1, 0)])  1.13 us
  transfers between devices with their start and end apart: 1, of which 1 were waited for; matrix products, arithmetic and copies ran while one was open for 0% of the time, Pallas kernels for 0%

profile of v5, /device:TPU:1, one launch (start us, length us, event | category | flops | bytes accessed | tf_op | source)
XLA Modules:
  0.0 44.4 jit_solution(9951194481714672845)
XLA Ops:
  0.0 0.0 copy-start.2
  0.0 0.0 copy-start
  0.0 0.0 copy-start.1
  0.0 1.9 %attend.1 = (f32[24,128]{1,0:T(8,128)S(1)}, f32[4,8]{1,0:T(4,128)S(1)}) custom-call(s32[4]{0:T(128)} %lengths.1, bf16[1,3072]{1,0:T(2,128)(2,1)} %queries.1, bf16[1,512,512]{2,1,0:T(8,128)(2,1)} %key_rows.1, bf16[1,512,512]{2,1,0:T(8,128)(2,1)} %value_rows.1, bf16[1,512]{1,0:T(2,128)(2,1)} %new_keys.1, bf16[1,512]{1,0:T(2,128)(2,1)} %new_values.1, ...), custom_call_target="tpu_custom_call" | custom-call | flops 40000000000 | tf_op jit(solution)/shard_map/attend/pallas_call | solution.py:134
  2.0 0.1 collective-permute-start
  2.1 1.1 %collective-permute-done.other = f32[24,128]{1,0:T(8,128)S(1)} collective-permute-done((f32[24,128]{1,0:T(8,128)S(1)}, f32[24,128]{1,0:T(8,128)S(1)}, u32[]{:S(2)}, u32[]{:S(2)}) %collective-permute-start) | collective-permute-done | bytes 12320 | tf_op jit(solution)/shard_map/ppermute | solution.py:394
  3.2 0.0 copy-done.2
  3.2 0.1 norm.1
  3.3 14.8 %all_to_all.10.parts = bf16[16,48,128]{2,1,0:T(8,128)(2,1)S(1)} all-to-all(bf16[16,48,128]{2,1,0:T(8,128)(2,1)S(1)} %norm.1), channel_id=1, replica_groups=mesh['grp'=4,'pair'=4,'half'=2] {'grp','pair'}, dimensions={0} | all-to-all | bytes 393216 | tf_op jit(solution)/shard_map/all_to_all | solution.py:396
  18.1 0.0 copy-done
  18.1 0.0 copy-done.1
  18.1 10.8 %experts.1 = bf16[32,4,768]{2,1,0:T(4,128)(2,1)} custom-call(bf16[16,48,128]{2,1,0:T(8,128)(2,1)S(1)} %all_to_all.10.parts, bf16[6144,2048]{1,0:T(8,128)(2,1)S(1)} %copy-done, bf16[6144,2048]{1,0:T(8,128)(2,1)S(1)} %copy-done.1, bf16[2048,6144]{1,0:T(8,128)(2,1)} %w_down.1), custom_call_target="tpu_custom_call" | custom-call | tf_op jit(solution)/shard_map/experts/pallas_call | solution.py:318
  28.9 14.8 %all_to_all.11.parts = bf16[32,4,768]{2,1,0:T(4,128)(2,1)S(1)} all-to-all(bf16[32,4,768]{2,1,0:T(4,128)(2,1)} %experts.1), channel_id=1, replica_groups=mesh['grp'=4,'pair'=4,'half'=2] {'grp','pair','half'}, dimensions={0} | all-to-all | bytes 393216 | tf_op jit(solution)/shard_map/all_to_all | solution.py:400
  43.7 0.7 %combine.1 = bf16[4,768]{1,0:T(4,128)(2,1)} custom-call(bf16[32,4,768]{2,1,0:T(4,128)(2,1)S(1)} %all_to_all.11.parts, f32[4,8]{1,0:T(4,128)S(1)} %get-tuple-element.8.weights), custom_call_target="tpu_custom_call" | custom-call | tf_op jit(solution)/shard_map/combine/pallas_call | solution.py:362
Async XLA Ops:
  0.0 3.2 %copy-start.2 = (f32[6144]{0:T(1024)S(1)}, f32[6144]{0:T(1024)}, u32[]{:S(2)}) copy-start(f32[6144]{0:T(1024)} %param.20) | copy-start | bytes 73732
  0.0 18.1 %copy-start = (bf16[6144,2048]{1,0:T(8,128)(2,1)S(1)}, bf16[6144,2048]{1,0:T(8,128)(2,1)}, u32[]{:S(2)}) copy-start(bf16[6144,2048]{1,0:T(8,128)(2,1)} %w_gate.1) | copy-start | bytes 75497472
  0.0 18.1 %copy-start.1 = (bf16[6144,2048]{1,0:T(8,128)(2,1)S(1)}, bf16[6144,2048]{1,0:T(8,128)(2,1)}, u32[]{:S(2)}) copy-start(bf16[6144,2048]{1,0:T(8,128)(2,1)} %w_up.1) | copy-start | bytes 75497472
  2.0 1.2 %collective-permute-start = (f32[24,128]{1,0:T(8,128)S(1)}, f32[24,128]{1,0:T(8,128)S(1)}, u32[]{:S(2)}, u32[]{:S(2)}) collective-permute-start(f32[24,128]{1,0:T(8,128)S(1)} %get-tuple-element.7.mine), channel_id=1, source_target_pairs={{0,1},{1,0},{2,3},{3,2},{4,5},{5,4},{6,7},{7,6},{8,9},{9,8},{10,11... | collective-permute-start | bytes 36872 | tf_op jit(solution)/shard_map/ppermute | solution.py:394

commit v6 on v5

--- a/solution.py
+++ b/solution.py
@@ -1,4 +1,5 @@
 import functools
+import math
 
 import jax
 import jax.numpy as jnp
@@ -158,26 +159,26 @@
 
 
 def norm_kernel(mine, other, gain, out):
-    first = lax.axis_index("half") == 0
-    row = jnp.concatenate(
-        [jnp.where(first, mine[...], other[...]), jnp.where(first, other[...], mine[...])], axis=0
-    )
-    square = jnp.sum(jnp.sum(row * row, axis=0, keepdims=True), axis=1, keepdims=True)
-    inverse = lax.rsqrt(square * (1.0 / (row.shape[0] * HEAD_SIZE)) + 1e-05)
-    normed = (row * inverse * gain[...]).astype(jnp.bfloat16)
+    heads = mine.shape[0]
+    own = mine[...]
+    square = jnp.sum(own * own + other[...] * other[...], axis=0, keepdims=True)
+    square = jnp.sum(square, axis=1, keepdims=True)
+    inverse = lax.rsqrt(square * (1.0 / (SHARING_DEVICES * heads * HEAD_SIZE)) + 1e-05)
+    at = pl.ds(pl.multiple_of(lax.axis_index("half") * heads, 8), heads)
+    normed = (own * inverse * gain[at, :]).astype(jnp.bfloat16)
     out[...] = jnp.broadcast_to(normed[None], out.shape)
 
 
-def norm(mine, other, gain, chips):
-    heads = gain.shape[0] // HEAD_SIZE
+def norm(mine, other, gain, devices):
+    shape = (devices,) + mine.shape
     return pl.pallas_call(
         norm_kernel,
-        out_shape=jax.ShapeDtypeStruct((chips, heads, HEAD_SIZE), jnp.bfloat16),
+        out_shape=jax.ShapeDtypeStruct(shape, jnp.bfloat16),
         in_specs=[VMEM] * 3,
         out_specs=VMEM,
-        compiler_params=pltpu.CompilerParams(vmem_limit_bytes=MIB + 4 * chips * gain.shape[0]),
+        compiler_params=pltpu.CompilerParams(vmem_limit_bytes=MIB + 2 * math.prod(shape)),
         name="norm",
-    )(mine, other, gain.reshape(heads, HEAD_SIZE))
+    )(mine, other, gain.reshape(-1, HEAD_SIZE))
 
 
 class Job:
@@ -311,13 +312,14 @@
 
 
 def experts(parts, w_gate, w_up, w_down, group_rows, dev_count):
-    tokens = parts.shape[0]
+    devices = parts.shape[0]
     width, local_hidden = w_gate.shape
+    tokens = devices // SHARING_DEVICES
     columns = width // dev_count
     units = local_hidden // PASSES
     return pl.pallas_call(
         experts_kernel,
-        out_shape=jax.ShapeDtypeStruct((SHARING_DEVICES * tokens, group_rows, columns), jnp.bfloat16),
+        out_shape=jax.ShapeDtypeStruct((devices, group_rows, columns), jnp.bfloat16),
         in_specs=[VMEM, VMEM, VMEM, HBM],
         out_specs=VMEM,
         scratch_shapes=[
@@ -384,7 +386,6 @@
     w_up,
     w_down,
 ):
-    chips = lax.axis_size("grp") * lax.axis_size("pair")
     dev_count = lax.axis_size("pair") * SHARING_DEVICES
     group_rows = residual.shape[0]
     summed, weights = attend(
@@ -392,8 +393,8 @@
         residual, expert_ids, route_logits,
     )
     other = lax.ppermute(summed, "half", [(0, 1), (1, 0)])
-    sent = norm(summed, other, norm_gain, chips)
-    rows = lax.all_to_all(sent, ("grp", "pair"), 0, 0, tiled=True)
+    sent = norm(summed, other, norm_gain, lax.axis_size("grp") * dev_count)
+    rows = lax.all_to_all(sent, ("grp", "pair", "half"), 0, 0, tiled=True)
     whole_blocks = w_gate.shape[1] % (PASSES * TILE) == 0 and norm_gain.shape[0] // dev_count % PART == 0
     run_experts = experts if whole_blocks else experts_plain
     part = run_experts(rows, w_gate, w_up, w_down, group_rows, dev_count)

time: 44.6 us -> 43.8 us (0.982)
  blocking collectives: 29.6 us -> 28.8 us
    all_to_all x1, blocking collectives: 14.8 us -> 12.6 us  [body(): got = lax.all_to_all(part, ('grp', 'pair', 'half'), 0, 0, tiled=True)]
    all_to_all x1, blocking collectives: 14.8 us -> 16.2 us  [body(): rows = lax.all_to_all(sent, ('grp', 'pair', 'half'), 0, 0, tiled=True)]
where the time goes in v6:
time: 43.8 us; the launch traced here: 43.6 us
  blocking collectives  28.8 us (66%)
  Pallas kernels  13.5 us (31%)
  waiting for transfers between devices  1.13 us (3%)
    all_to_all x1, blocking collectives, body(): rows = lax.all_to_all(sent, ('grp', 'pair', 'half'), 0, 0, tiled=True)  16.2 us
    all_to_all x1, blocking collectives, body(): got = lax.all_to_all(part, ('grp', 'pair', 'half'), 0, 0, tiled=True)  12.6 us
    pallas_call x1, Pallas kernels, experts(): pl.pallas_call(experts_kernel, out_shape=jax.ShapeDtypeStruct((devices, g...  10.8 us
    pallas_call x1, Pallas kernels, attend(): pl.pallas_call(attend_kernel, out_shape=(jax.ShapeDtypeStruct((LOCAL_HEAD...  1.93 us
    ppermute x1, waiting for transfers between devices, body(): other = lax.ppermute(summed, 'half', [(0, 1), (1, 0)])  1.13 us
  transfers between devices with their start and end apart: 1, of which 1 were waited for; matrix products, arithmetic and copies ran while one was open for 0% of the time, Pallas kernels for 0%

profile of v6, /device:TPU:1, one launch (start us, length us, event | category | flops | bytes accessed | tf_op | source)
XLA Modules:
  0.0 43.6 jit_solution(15337223448015589895)
XLA Ops:
  0.0 0.0 copy-start.2
  0.0 0.0 copy-start
  0.0 0.0 copy-start.1
  0.0 1.9 %attend.1 = (f32[24,128]{1,0:T(8,128)S(1)}, f32[4,8]{1,0:T(4,128)S(1)}) custom-call(s32[4]{0:T(128)} %lengths.1, bf16[1,3072]{1,0:T(2,128)(2,1)} %queries.1, bf16[1,512,512]{2,1,0:T(8,128)(2,1)} %key_rows.1, bf16[1,512,512]{2,1,0:T(8,128)(2,1)} %value_rows.1, bf16[1,512]{1,0:T(2,128)(2,1)} %new_keys.1, bf16[1,512]{1,0:T(2,128)(2,1)} %new_values.1, ...), custom_call_target="tpu_custom_call" | custom-call | flops 40000000000 | tf_op jit(solution)/shard_map/attend/pallas_call | solution.py:135
  2.0 0.1 collective-permute-start
  2.1 1.1 %collective-permute-done.other = f32[24,128]{1,0:T(8,128)S(1)} collective-permute-done((f32[24,128]{1,0:T(8,128)S(1)}, f32[24,128]{1,0:T(8,128)S(1)}, u32[]{:S(2)}, u32[]{:S(2)}) %collective-permute-start) | collective-permute-done | bytes 12320 | tf_op jit(solution)/shard_map/ppermute | solution.py:395
  3.2 0.0 copy-done.2
  3.2 0.1 norm.1
  3.3 16.2 %all_to_all.10.parts = bf16[32,24,128]{2,1,0:T(8,128)(2,1)S(1)} all-to-all(bf16[32,24,128]{2,1,0:T(8,128)(2,1)S(1)} %norm.1), channel_id=1, replica_groups=mesh['grp'=4,'pair'=4,'half'=2] {'grp','pair','half'}, dimensions={0} | all-to-all | bytes 393216 | tf_op jit(solution)/shard_map/all_to_all | solution.py:397
  19.5 0.0 copy-done
  19.5 0.0 copy-done.1
  19.5 10.8 %experts.1 = bf16[32,4,768]{2,1,0:T(4,128)(2,1)} custom-call(bf16[32,24,128]{2,1,0:T(8,128)(2,1)S(1)} %all_to_all.10.parts, bf16[6144,2048]{1,0:T(8,128)(2,1)S(1)} %copy-done, bf16[6144,2048]{1,0:T(8,128)(2,1)S(1)} %copy-done.1, bf16[2048,6144]{1,0:T(8,128)(2,1)} %w_down.1), custom_call_target="tpu_custom_call" | custom-call | tf_op jit(solution)/shard_map/experts/pallas_call | solution.py:320
  30.3 12.6 %all_to_all.11.parts = bf16[32,4,768]{2,1,0:T(4,128)(2,1)S(1)} all-to-all(bf16[32,4,768]{2,1,0:T(4,128)(2,1)} %experts.1), channel_id=1, replica_groups=mesh['grp'=4,'pair'=4,'half'=2] {'grp','pair','half'}, dimensions={0} | all-to-all | bytes 393216 | tf_op jit(solution)/shard_map/all_to_all | solution.py:401
  42.9 0.7 %combine.1 = bf16[4,768]{1,0:T(4,128)(2,1)} custom-call(bf16[32,4,768]{2,1,0:T(4,128)(2,1)S(1)} %all_to_all.11.parts, f32[4,8]{1,0:T(4,128)S(1)} %get-tuple-element.8.weights), custom_call_target="tpu_custom_call" | custom-call | tf_op jit(solution)/shard_map/combine/pallas_call | solution.py:364
Async XLA Ops:
  0.0 3.2 %copy-start.2 = (f32[6144]{0:T(1024)S(1)}, f32[6144]{0:T(1024)}, u32[]{:S(2)}) copy-start(f32[6144]{0:T(1024)} %param.20) | copy-start | bytes 73732
  0.0 19.5 %copy-start = (bf16[6144,2048]{1,0:T(8,128)(2,1)S(1)}, bf16[6144,2048]{1,0:T(8,128)(2,1)}, u32[]{:S(2)}) copy-start(bf16[6144,2048]{1,0:T(8,128)(2,1)} %w_gate.1) | copy-start | bytes 75497472
  0.0 19.5 %copy-start.1 = (bf16[6144,2048]{1,0:T(8,128)(2,1)S(1)}, bf16[6144,2048]{1,0:T(8,128)(2,1)}, u32[]{:S(2)}) copy-start(bf16[6144,2048]{1,0:T(8,128)(2,1)} %w_up.1) | copy-start | bytes 75497472
  2.0 1.2 %collective-permute-start = (f32[24,128]{1,0:T(8,128)S(1)}, f32[24,128]{1,0:T(8,128)S(1)}, u32[]{:S(2)}, u32[]{:S(2)}) collective-permute-start(f32[24,128]{1,0:T(8,128)S(1)} %get-tuple-element.7.mine), channel_id=1, source_target_pairs={{0,1},{1,0},{2,3},{3,2},{4,5},{5,4},{6,7},{7,6},{8,9},{9,8},{10,11... | collective-permute-start | bytes 36872 | tf_op jit(solution)/shard_map/ppermute | solution.py:395

commit v7 on v6

--- a/solution.py
+++ b/solution.py
@@ -319,7 +319,7 @@
     units = local_hidden // PASSES
     return pl.pallas_call(
         experts_kernel,
-        out_shape=jax.ShapeDtypeStruct((devices, group_rows, columns), jnp.bfloat16),
+        out_shape=pltpu.VMEM((devices, group_rows, columns), jnp.bfloat16),
         in_specs=[VMEM, VMEM, VMEM, HBM],
         out_specs=VMEM,
         scratch_shapes=[

time: 43.8 us -> 42.9 us (0.979)
  Pallas kernels: 13.5 us -> 12.8 us
    pallas_call x1, Pallas kernels: 10.8 us -> 10.1 us  [experts(): pl.pallas_call(experts_kernel, out_shape=pltpu.VMEM((devices, group_rows,...]
where the time goes in v7:
time: 42.9 us; the launch traced here: 42.7 us
  blocking collectives  28.6 us (67%)
  Pallas kernels  12.8 us (30%)
  waiting for transfers between devices  1.13 us (3%)
    all_to_all x1, blocking collectives, body(): rows = lax.all_to_all(sent, ('grp', 'pair', 'half'), 0, 0, tiled=True)  16.2 us
    all_to_all x1, blocking collectives, body(): got = lax.all_to_all(part, ('grp', 'pair', 'half'), 0, 0, tiled=True)  12.4 us
    pallas_call x1, Pallas kernels, experts(): pl.pallas_call(experts_kernel, out_shape=pltpu.VMEM((devices, group_rows,...  10.1 us
    pallas_call x1, Pallas kernels, attend(): pl.pallas_call(attend_kernel, out_shape=(jax.ShapeDtypeStruct((LOCAL_HEAD...  1.93 us
    ppermute x1, waiting for transfers between devices, body(): other = lax.ppermute(summed, 'half', [(0, 1), (1, 0)])  1.13 us
  transfers between devices with their start and end apart: 1, of which 1 were waited for; matrix products, arithmetic and copies ran while one was open for 0% of the time, Pallas kernels for 0%

profile of v7, /device:TPU:1, one launch (start us, length us, event | category | flops | bytes accessed | tf_op | source)
XLA Modules:
  0.0 42.7 jit_solution(13864858375921135052)
XLA Ops:
  0.0 0.0 copy-start.2
  0.0 0.0 copy-start
  0.0 0.0 copy-start.1
  0.0 1.9 %attend.1 = (f32[24,128]{1,0:T(8,128)S(1)}, f32[4,8]{1,0:T(4,128)S(1)}) custom-call(s32[4]{0:T(128)} %lengths.1, bf16[1,3072]{1,0:T(2,128)(2,1)} %queries.1, bf16[1,512,512]{2,1,0:T(8,128)(2,1)} %key_rows.1, bf16[1,512,512]{2,1,0:T(8,128)(2,1)} %value_rows.1, bf16[1,512]{1,0:T(2,128)(2,1)} %new_keys.1, bf16[1,512]{1,0:T(2,128)(2,1)} %new_values.1, ...), custom_call_target="tpu_custom_call" | custom-call | flops 40000000000 | tf_op jit(solution)/shard_map/attend/pallas_call | solution.py:135
  2.0 0.1 collective-permute-start
  2.1 1.1 %collective-permute-done.other = f32[24,128]{1,0:T(8,128)S(1)} collective-permute-done((f32[24,128]{1,0:T(8,128)S(1)}, f32[24,128]{1,0:T(8,128)S(1)}, u32[]{:S(2)}, u32[]{:S(2)}) %collective-permute-start) | collective-permute-done | bytes 12320 | tf_op jit(solution)/shard_map/ppermute | solution.py:395
  3.2 0.0 copy-done.2
  3.2 0.1 norm.1
  3.3 16.2 %all_to_all.10.parts = bf16[32,24,128]{2,1,0:T(8,128)(2,1)S(1)} all-to-all(bf16[32,24,128]{2,1,0:T(8,128)(2,1)S(1)} %norm.1), channel_id=1, replica_groups=mesh['grp'=4,'pair'=4,'half'=2] {'grp','pair','half'}, dimensions={0} | all-to-all | bytes 393216 | tf_op jit(solution)/shard_map/all_to_all | solution.py:397
  19.5 0.0 copy-done
  19.5 0.0 copy-done.1
  19.5 10.1 %experts.1 = bf16[32,4,768]{2,1,0:T(4,128)(2,1)S(1)} custom-call(bf16[32,24,128]{2,1,0:T(8,128)(2,1)S(1)} %all_to_all.10.parts, bf16[6144,2048]{1,0:T(8,128)(2,1)S(1)} %copy-done, bf16[6144,2048]{1,0:T(8,128)(2,1)S(1)} %copy-done.1, bf16[2048,6144]{1,0:T(8,128)(2,1)} %w_down.1), custom_call_target="tpu_custom_call" | custom-call | tf_op jit(solution)/shard_map/experts/pallas_call | solution.py:320
  29.6 12.4 %all_to_all.11.parts = bf16[32,4,768]{2,1,0:T(4,128)(2,1)S(1)} all-to-all(bf16[32,4,768]{2,1,0:T(4,128)(2,1)S(1)} %experts.1), channel_id=1, replica_groups=mesh['grp'=4,'pair'=4,'half'=2] {'grp','pair','half'}, dimensions={0} | all-to-all | bytes 393216 | tf_op jit(solution)/shard_map/all_to_all | solution.py:401
  42.0 0.7 %combine.1 = bf16[4,768]{1,0:T(4,128)(2,1)} custom-call(bf16[32,4,768]{2,1,0:T(4,128)(2,1)S(1)} %all_to_all.11.parts, f32[4,8]{1,0:T(4,128)S(1)} %get-tuple-element.8.weights), custom_call_target="tpu_custom_call" | custom-call | tf_op jit(solution)/shard_map/combine/pallas_call | solution.py:364
Async XLA Ops:
  0.0 3.2 %copy-start.2 = (f32[6144]{0:T(1024)S(1)}, f32[6144]{0:T(1024)}, u32[]{:S(2)}) copy-start(f32[6144]{0:T(1024)} %param.20) | copy-start | bytes 73732
  0.0 19.5 %copy-start = (bf16[6144,2048]{1,0:T(8,128)(2,1)S(1)}, bf16[6144,2048]{1,0:T(8,128)(2,1)}, u32[]{:S(2)}) copy-start(bf16[6144,2048]{1,0:T(8,128)(2,1)} %w_gate.1) | copy-start | bytes 75497472
  0.0 19.5 %copy-start.1 = (bf16[6144,2048]{1,0:T(8,128)(2,1)S(1)}, bf16[6144,2048]{1,0:T(8,128)(2,1)}, u32[]{:S(2)}) copy-start(bf16[6144,2048]{1,0:T(8,128)(2,1)} %w_up.1) | copy-start | bytes 75497472
  2.0 1.2 %collective-permute-start = (f32[24,128]{1,0:T(8,128)S(1)}, f32[24,128]{1,0:T(8,128)S(1)}, u32[]{:S(2)}, u32[]{:S(2)}) collective-permute-start(f32[24,128]{1,0:T(8,128)S(1)} %get-tuple-element.7.mine), channel_id=1, source_target_pairs={{0,1},{1,0},{2,3},{3,2},{4,5},{5,4},{6,7},{7,6},{8,9},{9,8},{10,11... | collective-permute-start | bytes 36872 | tf_op jit(solution)/shard_map/ppermute | solution.py:395

commit v8 on v7

--- a/solution.py
+++ b/solution.py
@@ -239,7 +239,7 @@
     for i in range(min(slots, PASSES * blocks)):
         down_copy(i).start()
 
-    flat[...] = parts[...].astype(jnp.float32).reshape(flat.shape)
+    flat[: tokens * heads, :] = parts[...].astype(jnp.float32).reshape(tokens * heads, HEAD_SIZE)
     for j in range(heads):
         normed[:, j * HEAD_SIZE : (j + 1) * HEAD_SIZE] = flat[
             pl.ds(j, tokens, stride=heads), :
@@ -323,7 +323,7 @@
         in_specs=[VMEM, VMEM, VMEM, HBM],
         out_specs=VMEM,
         scratch_shapes=[
-            pltpu.VMEM((tokens * width // HEAD_SIZE, HEAD_SIZE), jnp.float32),
+            pltpu.VMEM(((tokens + 1) * width // HEAD_SIZE, HEAD_SIZE), jnp.float32),
             pltpu.VMEM((tokens, width), jnp.bfloat16),
             pltpu.VMEM((tokens, local_hidden), jnp.bfloat16),
             pltpu.VMEM((tokens, 2 * MXU), jnp.float32),

time: 42.9 us -> 42.8 us (level)
  no operation moved by 1% of the time
where the time goes in v8:
time: 42.8 us; the launch traced here: 42.7 us
  blocking collectives  28.6 us (67%)
  Pallas kernels  12.8 us (30%)
  waiting for transfers between devices  1.13 us (3%)
    all_to_all x1, blocking collectives, body(): rows = lax.all_to_all(sent, ('grp', 'pair', 'half'), 0, 0, tiled=True)  16.2 us
    all_to_all x1, blocking collectives, body(): got = lax.all_to_all(part, ('grp', 'pair', 'half'), 0, 0, tiled=True)  12.4 us
    pallas_call x1, Pallas kernels, experts(): pl.pallas_call(experts_kernel, out_shape=pltpu.VMEM((devices, group_rows,...  10.1 us
    pallas_call x1, Pallas kernels, attend(): pl.pallas_call(attend_kernel, out_shape=(jax.ShapeDtypeStruct((LOCAL_HEAD...  1.93 us
    ppermute x1, waiting for transfers between devices, body(): other = lax.ppermute(summed, 'half', [(0, 1), (1, 0)])  1.13 us
  transfers between devices with their start and end apart: 1, of which 1 were waited for; matrix products, arithmetic and copies ran while one was open for 0% of the time, Pallas kernels for 0%

profile of v8, /device:TPU:1, one launch (start us, length us, event | category | flops | bytes accessed | tf_op | source)
XLA Modules:
  0.0 42.7 jit_solution(15939099497675073850)
XLA Ops:
  0.0 0.0 copy-start.2
  0.0 0.0 copy-start
  0.0 0.0 copy-start.1
  0.0 1.9 %attend.1 = (f32[24,128]{1,0:T(8,128)S(1)}, f32[4,8]{1,0:T(4,128)S(1)}) custom-call(s32[4]{0:T(128)} %lengths.1, bf16[1,3072]{1,0:T(2,128)(2,1)} %queries.1, bf16[1,512,512]{2,1,0:T(8,128)(2,1)} %key_rows.1, bf16[1,512,512]{2,1,0:T(8,128)(2,1)} %value_rows.1, bf16[1,512]{1,0:T(2,128)(2,1)} %new_keys.1, bf16[1,512]{1,0:T(2,128)(2,1)} %new_values.1, ...), custom_call_target="tpu_custom_call" | custom-call | flops 40000000000 | tf_op jit(solution)/shard_map/attend/pallas_call | solution.py:135
  2.0 0.1 collective-permute-start
  2.1 1.1 %collective-permute-done.other = f32[24,128]{1,0:T(8,128)S(1)} collective-permute-done((f32[24,128]{1,0:T(8,128)S(1)}, f32[24,128]{1,0:T(8,128)S(1)}, u32[]{:S(2)}, u32[]{:S(2)}) %collective-permute-start) | collective-permute-done | bytes 12320 | tf_op jit(solution)/shard_map/ppermute | solution.py:395
  3.2 0.0 copy-done.2
  3.2 0.1 norm.1
  3.3 16.2 %all_to_all.10.parts = bf16[32,24,128]{2,1,0:T(8,128)(2,1)S(1)} all-to-all(bf16[32,24,128]{2,1,0:T(8,128)(2,1)S(1)} %norm.1), channel_id=1, replica_groups=mesh['grp'=4,'pair'=4,'half'=2] {'grp','pair','half'}, dimensions={0} | all-to-all | bytes 393216 | tf_op jit(solution)/shard_map/all_to_all | solution.py:397
  19.5 0.0 copy-done
  19.5 0.0 copy-done.1
  19.5 10.1 %experts.1 = bf16[32,4,768]{2,1,0:T(4,128)(2,1)S(1)} custom-call(bf16[32,24,128]{2,1,0:T(8,128)(2,1)S(1)} %all_to_all.10.parts, bf16[6144,2048]{1,0:T(8,128)(2,1)S(1)} %copy-done, bf16[6144,2048]{1,0:T(8,128)(2,1)S(1)} %copy-done.1, bf16[2048,6144]{1,0:T(8,128)(2,1)} %w_down.1), custom_call_target="tpu_custom_call" | custom-call | tf_op jit(solution)/shard_map/experts/pallas_call | solution.py:320
  29.6 12.4 %all_to_all.11.parts = bf16[32,4,768]{2,1,0:T(4,128)(2,1)S(1)} all-to-all(bf16[32,4,768]{2,1,0:T(4,128)(2,1)S(1)} %experts.1), channel_id=1, replica_groups=mesh['grp'=4,'pair'=4,'half'=2] {'grp','pair','half'}, dimensions={0} | all-to-all | bytes 393216 | tf_op jit(solution)/shard_map/all_to_all | solution.py:401
  42.0 0.7 %combine.1 = bf16[4,768]{1,0:T(4,128)(2,1)} custom-call(bf16[32,4,768]{2,1,0:T(4,128)(2,1)S(1)} %all_to_all.11.parts, f32[4,8]{1,0:T(4,128)S(1)} %get-tuple-element.8.weights), custom_call_target="tpu_custom_call" | custom-call | tf_op jit(solution)/shard_map/combine/pallas_call | solution.py:364
Async XLA Ops:
  0.0 3.2 %copy-start.2 = (f32[6144]{0:T(1024)S(1)}, f32[6144]{0:T(1024)}, u32[]{:S(2)}) copy-start(f32[6144]{0:T(1024)} %param.20) | copy-start | bytes 73732
  0.0 19.5 %copy-start = (bf16[6144,2048]{1,0:T(8,128)(2,1)S(1)}, bf16[6144,2048]{1,0:T(8,128)(2,1)}, u32[]{:S(2)}) copy-start(bf16[6144,2048]{1,0:T(8,128)(2,1)} %w_gate.1) | copy-start | bytes 75497472
  0.0 19.5 %copy-start.1 = (bf16[6144,2048]{1,0:T(8,128)(2,1)S(1)}, bf16[6144,2048]{1,0:T(8,128)(2,1)}, u32[]{:S(2)}) copy-start(bf16[6144,2048]{1,0:T(8,128)(2,1)} %w_up.1) | copy-start | bytes 75497472
  2.0 1.2 %collective-permute-start = (f32[24,128]{1,0:T(8,128)S(1)}, f32[24,128]{1,0:T(8,128)S(1)}, u32[]{:S(2)}, u32[]{:S(2)}) collective-permute-start(f32[24,128]{1,0:T(8,128)S(1)} %get-tuple-element.7.mine), channel_id=1, source_target_pairs={{0,1},{1,0},{2,3},{3,2},{4,5},{5,4},{6,7},{7,6},{8,9},{9,8},{10,11... | collective-permute-start | bytes 36872 | tf_op jit(solution)/shard_map/ppermute | solution.py:395

commit v9 on v8

--- a/solution.py
+++ b/solution.py
@@ -24,6 +24,7 @@
 RING = 6
 PASSES = 2
 DOWN = 1024
+CACHE_PARTS = 4
 UNTIL_ROWS = pl.CostEstimate(flops=40_000_000_000, bytes_accessed=0, transcendentals=0)
 
 
@@ -56,23 +57,33 @@
     columns = heads * HEAD_SIZE
     at = pl.ds(pl.multiple_of(half * columns, HEAD_SIZE), columns)
     pairs = [
-        (key_rows.at[0], key_buf),
         (queries, query_buf),
         (new_keys, new_key_buf),
         (lengths, length_buf),
         (new_values, new_value_buf),
-        (value_rows.at[0], value_buf),
         (residual.at[:, at], residual_buf),
         (ids, id_buf),
         (logits, logit_buf),
     ]
     copies = [pltpu.make_async_copy(*pair, sems.at[i]) for i, pair in enumerate(pairs)]
-    for copy in copies:
+    cache_len, width = key_buf.shape
+    step = cache_len // CACHE_PARTS
+
+    def cache_copies(source, target, first):
+        return [
+            pltpu.make_async_copy(
+                source.at[0, pl.ds(k * step, step)], target.at[pl.ds(k * step, step)], sems.at[first + k]
+            )
+            for k in range(CACHE_PARTS)
+        ]
+
+    key_copies = cache_copies(key_rows, key_buf, len(copies))
+    value_copies = cache_copies(value_rows, value_buf, len(copies) + CACHE_PARTS)
+    for copy in key_copies + copies + value_copies:
         copy.start()
-    cache_len, width = key_buf.shape
     kv_heads = width // HEAD_SIZE
     scale = HEAD_SIZE ** (-0.5)
-    for copy in copies[:4]:
+    for copy in key_copies + copies[:3]:
         copy.wait()
     query = head_rows(query_buf[...].astype(jnp.float32))
     owner = lax.broadcasted_iota(jnp.int32, (heads, HEAD_SIZE), 0) // GROUP_WIDTH
@@ -98,7 +109,7 @@
     denom = jnp.sum(exp_all, axis=1, keepdims=True) + exp_new
     weights = (exp_all / denom).astype(jnp.bfloat16)
     weight_new = (exp_new / denom).astype(jnp.bfloat16).astype(jnp.float32)
-    for copy in copies[4:]:
+    for copy in copies[3:] + value_copies:
         copy.wait()
     mixed = jnp.dot(weights, value_buf[...], preferred_element_type=jnp.float32)
     mixed = mixed + weight_new * new_value_buf[...].astype(jnp.float32)
@@ -150,7 +161,7 @@
             pltpu.VMEM((residual.shape[0], half_columns), jnp.bfloat16),
             pltpu.VMEM(ids.shape[::-1], jnp.int32),
             pltpu.VMEM(logits.shape[::-1], jnp.float32),
-            pltpu.SemaphoreType.DMA((len(operands),)),
+            pltpu.SemaphoreType.DMA((len(operands) - 2 + 2 * CACHE_PARTS,)),
         ],
         compiler_params=pltpu.CompilerParams(vmem_limit_bytes=4 * MIB),
         cost_estimate=UNTIL_ROWS,

time: 42.8 us -> 42.9 us (level)
  no operation moved by 1% of the time
where the time goes in v9:
time: 42.9 us; the launch traced here: 42.7 us
  blocking collectives  28.6 us (67%)
  Pallas kernels  12.9 us (30%)
  waiting for transfers between devices  1.13 us (3%)
    all_to_all x1, blocking collectives, body(): rows = lax.all_to_all(sent, ('grp', 'pair', 'half'), 0, 0, tiled=True)  16.2 us
    all_to_all x1, blocking collectives, body(): got = lax.all_to_all(part, ('grp', 'pair', 'half'), 0, 0, tiled=True)  12.4 us
    pallas_call x1, Pallas kernels, experts(): pl.pallas_call(experts_kernel, out_shape=pltpu.VMEM((devices, group_rows,...  10.1 us
    pallas_call x1, Pallas kernels, attend(): pl.pallas_call(attend_kernel, out_shape=(jax.ShapeDtypeStruct((LOCAL_HEAD...  2.04 us
    ppermute x1, waiting for transfers between devices, body(): other = lax.ppermute(summed, 'half', [(0, 1), (1, 0)])  1.13 us
  transfers between devices with their start and end apart: 1, of which 1 were waited for; matrix products, arithmetic and copies ran while one was open for 0% of the time, Pallas kernels for 0%

profile of v9, /device:TPU:1, one launch (start us, length us, event | category | flops | bytes accessed | tf_op | source)
XLA Modules:
  0.0 42.7 jit_solution(10569241299526539411)
XLA Ops:
  0.0 0.0 copy-start.2
  0.0 0.0 copy-start
  0.0 0.0 copy-start.1
  0.0 2.0 %attend.1 = (f32[24,128]{1,0:T(8,128)S(1)}, f32[4,8]{1,0:T(4,128)S(1)}) custom-call(s32[4]{0:T(128)} %lengths.1, bf16[1,3072]{1,0:T(2,128)(2,1)} %queries.1, bf16[1,512,512]{2,1,0:T(8,128)(2,1)} %key_rows.1, bf16[1,512,512]{2,1,0:T(8,128)(2,1)} %value_rows.1, bf16[1,512]{1,0:T(2,128)(2,1)} %new_keys.1, bf16[1,512]{1,0:T(2,128)(2,1)} %new_values.1, ...), custom_call_target="tpu_custom_call" | custom-call | flops 40000000000 | tf_op jit(solution)/shard_map/attend/pallas_call | solution.py:146
  2.1 0.1 collective-permute-start
  2.2 1.1 %collective-permute-done.other = f32[24,128]{1,0:T(8,128)S(1)} collective-permute-done((f32[24,128]{1,0:T(8,128)S(1)}, f32[24,128]{1,0:T(8,128)S(1)}, u32[]{:S(2)}, u32[]{:S(2)}) %collective-permute-start) | collective-permute-done | bytes 12320 | tf_op jit(solution)/shard_map/ppermute | solution.py:406
  3.3 0.0 copy-done.2
  3.3 0.1 norm.1
  3.4 16.2 %all_to_all.10.parts = bf16[32,24,128]{2,1,0:T(8,128)(2,1)S(1)} all-to-all(bf16[32,24,128]{2,1,0:T(8,128)(2,1)S(1)} %norm.1), channel_id=1, replica_groups=mesh['grp'=4,'pair'=4,'half'=2] {'grp','pair','half'}, dimensions={0} | all-to-all | bytes 393216 | tf_op jit(solution)/shard_map/all_to_all | solution.py:408
  19.6 0.0 copy-done
  19.6 0.0 copy-done.1
  19.6 10.1 %experts.1 = bf16[32,4,768]{2,1,0:T(4,128)(2,1)S(1)} custom-call(bf16[32,24,128]{2,1,0:T(8,128)(2,1)S(1)} %all_to_all.10.parts, bf16[6144,2048]{1,0:T(8,128)(2,1)S(1)} %copy-done, bf16[6144,2048]{1,0:T(8,128)(2,1)S(1)} %copy-done.1, bf16[2048,6144]{1,0:T(8,128)(2,1)} %w_down.1), custom_call_target="tpu_custom_call" | custom-call | tf_op jit(solution)/shard_map/experts/pallas_call | solution.py:331
  29.7 12.4 %all_to_all.11.parts = bf16[32,4,768]{2,1,0:T(4,128)(2,1)S(1)} all-to-all(bf16[32,4,768]{2,1,0:T(4,128)(2,1)S(1)} %experts.1), channel_id=1, replica_groups=mesh['grp'=4,'pair'=4,'half'=2] {'grp','pair','half'}, dimensions={0} | all-to-all | bytes 393216 | tf_op jit(solution)/shard_map/all_to_all | solution.py:412
  42.1 0.7 %combine.1 = bf16[4,768]{1,0:T(4,128)(2,1)} custom-call(bf16[32,4,768]{2,1,0:T(4,128)(2,1)S(1)} %all_to_all.11.parts, f32[4,8]{1,0:T(4,128)S(1)} %get-tuple-element.8.weights), custom_call_target="tpu_custom_call" | custom-call | tf_op jit(solution)/shard_map/combine/pallas_call | solution.py:375
Async XLA Ops:
  0.0 3.3 %copy-start.2 = (f32[6144]{0:T(1024)S(1)}, f32[6144]{0:T(1024)}, u32[]{:S(2)}) copy-start(f32[6144]{0:T(1024)} %param.20) | copy-start | bytes 73732
  0.0 19.6 %copy-start = (bf16[6144,2048]{1,0:T(8,128)(2,1)S(1)}, bf16[6144,2048]{1,0:T(8,128)(2,1)}, u32[]{:S(2)}) copy-start(bf16[6144,2048]{1,0:T(8,128)(2,1)} %w_gate.1) | copy-start | bytes 75497472
  0.0 19.6 %copy-start.1 = (bf16[6144,2048]{1,0:T(8,128)(2,1)S(1)}, bf16[6144,2048]{1,0:T(8,128)(2,1)}, u32[]{:S(2)}) copy-start(bf16[6144,2048]{1,0:T(8,128)(2,1)} %w_up.1) | copy-start | bytes 75497472
  2.1 1.2 %collective-permute-start = (f32[24,128]{1,0:T(8,128)S(1)}, f32[24,128]{1,0:T(8,128)S(1)}, u32[]{:S(2)}, u32[]{:S(2)}) collective-permute-start(f32[24,128]{1,0:T(8,128)S(1)} %get-tuple-element.7.mine), channel_id=1, source_target_pairs={{0,1},{1,0},{2,3},{3,2},{4,5},{5,4},{6,7},{7,6},{8,9},{9,8},{10,11... | collective-permute-start | bytes 36872 | tf_op jit(solution)/shard_map/ppermute | solution.py:406
